TPU v7x, 32 devices: a whole 2x2x4 slice. The times are simulated.
32 devices in a mesh: groups: 2 (over y), layer: 4 (over z), latent: 4 (over x, core).
Axes of the slice: x: 2, y: 2, z: 4, core: 2. Of those that a mesh axis runs over, the one named last changes fastest.
Arguments:
- residuals: bfloat16 [4, 256, 2304], P('layer', 'groups'), parts along dimension 1, may hold values from -6 to 6
- targets: bfloat16 [4, 256, 2304], P('layer', 'groups'), parts along dimension 1, may hold values from -6 to 6
- enc_weight: bfloat16 [4, 2304, 8192], P('layer', None, 'latent'), may hold values from -0.125 to 0.125
- enc_bias: float32 [4, 8192], P('layer', 'latent'), may hold values from -2.5 to 2.5
- dec_weight: bfloat16 [4, 8192, 2304], P('layer', 'latent'), may hold values from -0.0625 to 0.0625
- out_gain: float32 [4, 2304], P('layer'), may hold values from 0.1 to 1.9
- block_list: int32 [4, 2, 24], P('layer', 'groups'), parts along dimension 1, may hold values from 0 to 63, as said below
- block_count: int32 [4, 2], P('layer', 'groups'), parts along dimension 1, may hold values from 1 to 24
Outputs:
- recon: bfloat16 [4, 256, 2304], P('layer', 'groups', 'latent'), parts along dimension 1
- code_grad: bfloat16 [4, 256, 8192], P('layer', 'groups', 'latent'), parts along dimension 1
- layer_loss: float32 [2, 4], P('groups', 'layer'), parts along dimension 0
There are 2 independent parts, one for each index of `groups`. A program takes and returns all parts, laid end to end along the dimension named above; an argument that names none is the same for every part. Nothing has to cross between parts.
Inputs may be any that keep to these rules, and one draw needn't show every extreme that they name: `block_list`: within the first block_count entries of a row the blocks are distinct; later entries are unused.
All inputs are finite; a program needn't handle non-finite values.
Results may differ from a plain program's by a relative error of at most 0.0054.
Values may be sent and summed in bfloat16 or wider, within the bound.
No kernel may reach another device: no remote copies, remote signals or barrier semaphores. Data moves between devices by JAX's collectives and lax.ppermute only.
A program may use at most 128 MiB of HBM per device.

v0:
```python
import jax
import jax.numpy as jnp
from jax import lax
from jax.sharding import PartitionSpec as P

BLOCK = 128


def entering(value, axis, join, neutral, backward):
    count, mine = (lax.axis_size(axis), lax.axis_index(axis))
    pieces = lax.all_gather(value, axis)
    if backward:
        pieces = pieces[::-1]
        mine = count - 1 - mine
    total = jnp.full_like(value, 0) + jnp.asarray(neutral, value.dtype)

    def step(position, total):
        longer = join(total, pieces[position])
        return jnp.where(position < mine, longer, total)

    return lax.fori_loop(0, count - 1, step, total)


def add_terms(earlier, later):
    return earlier + later


def local(residuals, targets, enc_weight, enc_bias, dec_weight, out_gain, block_list, block_count):
    inputs = residuals[0]
    tok_rows, model_width = inputs.shape
    local_latents = enc_weight.shape[2]
    local_blocks = local_latents // BLOCK
    latent_index = lax.axis_index("latent")
    block_ids = latent_index * local_blocks + jnp.arange(local_blocks, dtype=jnp.int32)
    slot_count = block_list.shape[2]
    live_slots = jnp.arange(slot_count, dtype=jnp.int32)[None, :] < block_count[0][:, None]
    block_mask = jnp.any(
        (block_list[0][:, :, None] == block_ids[None, None, :]) & live_slots[:, :, None], axis=1
    ).astype(jnp.float32)
    tile_count = block_mask.shape[0]

    def masked(values):
        shaped = values.reshape(tile_count, tok_rows // tile_count, local_blocks, BLOCK)
        return (shaped * block_mask[:, None, :, None]).reshape(tok_rows, local_latents)

    pre_act = (
        jnp.dot(inputs, enc_weight[0], preferred_element_type=jnp.float32) + enc_bias[0][None, :]
    )
    latent_codes = masked(jnp.maximum(pre_act, 0.0)).astype(jnp.bfloat16)
    partial_value = jnp.dot(latent_codes, dec_weight[0], preferred_element_type=jnp.float32)
    latent_total = lax.psum(partial_value, "latent")
    before = entering(latent_total, "layer", add_terms, jnp.zeros_like(latent_total), False)
    summed = before + latent_total
    fitted = out_gain[0][None, :] * summed
    columns = model_width // lax.axis_size("latent")
    recon = lax.dynamic_slice_in_dim(
        fitted.astype(jnp.bfloat16), latent_index * columns, columns, 1
    )
    error_term = fitted - targets[0].astype(jnp.float32)
    loss_value = jnp.sum(error_term * error_term) / (tok_rows * model_width)
    backward = out_gain[0][None, :] * error_term
    suffix_part = entering(backward, "layer", add_terms, jnp.zeros_like(backward), True)
    grad_in = (suffix_part + backward).astype(jnp.bfloat16)
    grad_codes = lax.dot_general(
        grad_in, dec_weight[0], (((1,), (1,)), ((), ())), preferred_element_type=jnp.float32
    )
    code_grad = masked(grad_codes).astype(jnp.bfloat16)
    return (recon[None], code_grad[None], jnp.reshape(loss_value, (1, 1)).astype(jnp.float32))


def solution(mesh):
    placed = (
        P("layer", "groups", None),
        P("layer", "groups", None),
        P("layer", None, "latent"),
        P("layer", "latent"),
        P("layer", "latent", None),
        P("layer", None),
        P("layer", "groups", None),
        P("layer", "groups"),
    )
    return jax.shard_map(
        local,
        mesh=mesh,
        in_specs=placed,
        out_specs=(
            P("layer", "groups", "latent"),
            P("layer", "groups", "latent"),
            P("groups", "layer"),
        ),
        check_vma=False,
    )
```

profile of v0, /device:TPU:0, one launch (start us, length us, event | category | flops | bytes accessed | tf_op | source)
XLA Modules:
  0.0 271.8 jit_solution(6016291123703701460)
XLA Ops:
  7.2 0.0 all-reduce.2.cloned.1.call-start
  8.0 0.8 and_reduce_fusion
  8.8 0.1 broadcast_bitcast_fusion
  8.9 10.2 %fusion = f32[128,2304]{1,0:T(8,128)} fusion(bf16[1,2048,2304]{2,1,0:T(8,128)(2,1)} %param.16, bf16[1,2304,2048]{2,1,0:T(8,128)(2,1)} %param.14, bf16[1,128,2304]{2,1,0:T(8,128)(2,1)S(1)} %copy-done, f32[2048]{0:T(1024)S(1)} %broadcast_bitcast_fusion, f32[2048]{0:T(1024)} %bitcast.53), kind=kOutput, calls=%fused_computation.2 | convolution fusion | flops 2416967680 | bytes 20660224 | tf_op jit(solution)/shard_map/dot_general | solution.py:50
  19.1 0.0 all-gather.5.cloned.1.call-start
  19.2 40.2 %all-reduce.2.cloned.1.call-done = f32[128,2304]{1,0:T(8,128)} async-done(((f32[128,2304]{1,0:T(8,128)}), f32[128,2304]{1,0:T(8,128)}) %all-reduce.2.cloned.1.call-update) | async-done | bytes 1179664 | tf_op jit(solution)/shard_map/psum | solution.py:51
  59.4 0.0 all-gather.7.cloned.1.call-start
  59.5 91.0 %all-gather.5.cloned.1.call-done = f32[512,2304]{1,0:T(8,128)} async-done(((f32[128,2304]{1,0:T(8,128)}), f32[512,2304]{1,0:T(8,128)}) %all-gather.5.cloned.1.call-update) | async-done | bytes 4718608 | tf_op jit(solution)/shard_map/all_gather | solution.py:11
  150.5 5.0 %while.28 = (s32[]{:T(128)}, f32[128,2304]{1,0:T(8,128)S(1)}, s32[]{:T(128)}, f32[4,128,2304]{2,1,0:T(8,128)}, s32[]{:T(128)}, /*index=5*/s32[]{:T(128)}) while((s32[]{:T(128)}, f32[128,2304]{1,0:T(8,128)S(1)}, s32[]{:T(128)}, f32[4,128,2304]{2,1,0:T(8,128)}, s32[]{:T(128)}, /*index=5*/s32[]{:T(128)}) %tuple.79), condition=%wide.region_3.4_spmd.clone, body=%wide.region_2.3_spmd.clone.sunk | while | flops 884740 | bytes 3539037 | solution.py:21
  150.5 1.7 add_select_fusion.4
  152.2 1.6 add_select_fusion.4
  153.9 1.6 add_select_fusion.4
  155.5 2.2 multiply_reduce_fusion
  157.7 1.1 fusion.17
  158.9 0.1 dynamic-slice_convert_fusion
  159.0 0.8 copy.14
  160.4 86.4 %all-gather.7.cloned.1.call-done = f32[512,2304]{1,0:T(8,128)} async-done(((f32[128,2304]{1,0:T(8,128)}), f32[512,2304]{1,0:T(8,128)}) %all-gather.7.cloned.1.call-update) | async-done | bytes 4718608 | tf_op jit(solution)/shard_map/all_gather | solution.py:11
  246.9 4.9 %rev.3 = f32[4,128,2304]{2,1,0:T(8,128)} reverse(f32[4,128,2304]{2,1,0:T(8,128)} %bitcast.50), dimensions={0} | reverse | bytes 9437184 | tf_op jit(solution)/shard_map/rev | solution.py:13
  251.8 5.0 %while.29 = (s32[]{:T(128)}, f32[128,2304]{1,0:T(8,128)S(1)}, s32[]{:T(128)}, f32[4,128,2304]{2,1,0:T(8,128)}, s32[]{:T(128)}, /*index=5*/s32[]{:T(128)}) while((s32[]{:T(128)}, f32[128,2304]{1,0:T(8,128)S(1)}, s32[]{:T(128)}, f32[4,128,2304]{2,1,0:T(8,128)}, s32[]{:T(128)}, /*index=5*/s32[]{:T(128)}) %tuple.70), condition=%wide.region_5.6_spmd.clone, body=%wide.region_4.5_spmd.clone.sunk | while | flops 884740 | bytes 3539037 | solution.py:21
  251.8 1.7 add_select_fusion.5
  253.5 1.6 add_select_fusion.5
  255.2 1.6 add_select_fusion.5
  256.8 6.3 %fusion.16 = bf16[128,16,128]{0,2,1:T(8,128)(2,1)S(1)} fusion(bf16[16,128,2304]{2,1,0:T(8,128)(2,1)} %bitcast.48, f32[128,2304]{1,0:T(8,128)S(1)} %get-tuple-element.162, f32[128,2304]{1,0:T(8,128)S(1)} %copy-done.1, f32[16]{0:T(128)S(1)} %convert_element_type.37), kind=kOutput, calls=%fused_computation.11 | convolution fusion | flops 1209073664 | bytes 12320832 | tf_op jit(solution)/shard_map/dot_general | solution.py:64
  263.1 1.0 copy.15
  (17 shorter events, 0.1 us)
Async XLA Ops:
  7.2 1.7 copy-start
  7.2 52.2 %all-reduce.2.cloned.1.call-start = ((), (), s32[]{:S(2)}) async-start(), calls=%async_computation | async-start | bytes 2359296 | tf_op jit(solution)/shard_map/psum | solution.py:51
  19.1 40.3 %copy-start.3 = (f32[1,2304]{1,0:T(1,128)S(1)}, f32[1,2304]{1,0:T(1,128)}, u32[]{:S(2)}) copy-start(f32[1,2304]{1,0:T(1,128)} %param.17) | copy-start | bytes 27652
  19.1 131.4 %all-gather.5.cloned.1.call-start = ((), (), s32[]{:S(2)}) async-start(), calls=%async_computation.1 | async-start | bytes 5898240 | tf_op jit(solution)/shard_map/all_gather | solution.py:11
  59.4 187.5 %all-gather.7.cloned.1.call-start = ((), (), s32[]{:S(2)}) async-start(), calls=%async_computation.2 | async-start | bytes 5898240 | tf_op jit(solution)/shard_map/all_gather | solution.py:11
  150.5 5.0 %copy-start.2 = (bf16[1,128,2304]{2,1,0:T(8,128)(2,1)S(1)}, bf16[1,128,2304]{2,1,0:T(8,128)(2,1)}, u32[]{:S(2)}) copy-start(bf16[1,128,2304]{2,1,0:T(8,128)(2,1)} %param.13) | copy-start | bytes 1769476
  251.8 5.0 %copy-start.1 = (f32[128,2304]{1,0:T(8,128)S(1)}, f32[128,2304]{1,0:T(8,128)}, u32[]{:S(2)}) copy-start(f32[128,2304]{1,0:T(8,128)} %fusion.17) | copy-start | bytes 3538948
Sparse Core Ops, SparseCore 0:
  19.3 40.0 all-reduce.1
  60.9 89.5 all-gather.4
  159.0 87.8 all-gather.6
where the time goes:
time: 272 us
  waiting for transfers between devices  218 us (80%)
  matrix products  16.5 us (6%)
  between operations  16.3 us (6%)
  other arithmetic  14.1 us (5%)
  local copies, waits for them, and re-layouts  6.93 us (3%)
    all_gather x2, waiting for transfers between devices, entering(): pieces = lax.all_gather(value, axis)  177 us
    psum x1, waiting for transfers between devices, local(): latent_total = lax.psum(partial_value, 'latent')  40.2 us
    dot_general x1, matrix products, local(): jnp.dot(latent_codes, dec_weight[0], preferred_element_type=jnp.float32)  10.2 us
    select_n x6, other arithmetic, step(): return jnp.where(position < mine, longer, total)  9.86 us
    dot_general x1, matrix products, local(): lax.dot_general(grad_in, dec_weight[0], (((1,), (1,)), ((), ())), preferr...  6.3 us
  transfers between devices with their start and end apart: 3, of which 3 were waited for; matrix products, arithmetic and copies ran while one was open for 0% of the time, Pallas kernels for 0%

commit v1 on v0

v1 whole, which is shorter than its diff:
```python
import functools

import jax
import jax.numpy as jnp
from jax import lax
from jax.experimental import pallas as pl
from jax.experimental.pallas import tpu as pltpu
from jax.sharding import PartitionSpec as P

BLOCK = 128
PAIR = 2 * BLOCK
F32 = jnp.float32
BF16 = jnp.bfloat16


def encode_decode(list_ref, count_ref, x_ref, bias_ref, enc_ref, dec_ref, keep_ref, send_ref, dec_kept, ids_ref, enc_held, total, enc_sem, dec_sem):
    blocks = enc_ref.shape[1] // BLOCK
    where = lax.axis_index("latent")
    first = where * blocks
    slots = list_ref.shape[2]
    count = count_ref[0, 0]

    def copies(block, n):
        pair, half = lax.div(n, 2), lax.rem(n, 2) * BLOCK
        half = pl.multiple_of(half, BLOCK)
        start = pl.multiple_of(block * BLOCK, BLOCK)
        return (
            pltpu.make_async_copy(enc_ref.at[:, pl.ds(start, BLOCK)], enc_held.at[pair, :, pl.ds(half, BLOCK)], enc_sem.at[n]),
            pltpu.make_async_copy(dec_ref.at[pl.ds(start, BLOCK), :], dec_kept.at[pair, pl.ds(half, BLOCK), :], dec_sem.at[n]),
        )

    def look(slot, n):
        block = list_ref[0, 0, slot] - first
        live = (slot < count) & (block >= 0) & (block < blocks)

        @pl.when(live)
        def _():
            ids_ref[0, n] = block
            for copy in copies(block, n):
                copy.start()

        return n + live.astype(jnp.int32)

    live_count = lax.fori_loop(0, slots, look, jnp.int32(0))
    ids_ref[0, blocks] = live_count
    total[...] = jnp.zeros_like(total)
    pairs = lax.div(live_count + 1, 2)
    odd = lax.rem(live_count, 2) == 1

    @pl.when(odd)
    def _():
        dec_kept[pairs - 1, pl.ds(BLOCK, BLOCK), :] = jnp.zeros((BLOCK, dec_kept.shape[2]), BF16)
        ids_ref[0, live_count] = ids_ref[0, live_count - 1]

    def step(pair, carry):
        n = 2 * pair
        full = n + 1 < live_count
        one, two = ids_ref[0, n], ids_ref[0, n + 1]
        for copy in copies(one, n):
            copy.wait()

        @pl.when(full)
        def _():
            for copy in copies(two, n + 1):
                copy.wait()

        bias = jnp.concatenate(
            [bias_ref[:, pl.ds(pl.multiple_of(block * BLOCK, BLOCK), BLOCK)] for block in (one, two)], axis=1
        )
        pre_act = jnp.dot(x_ref[...], enc_held[pair], preferred_element_type=F32) + bias
        lane = lax.broadcasted_iota(jnp.int32, pre_act.shape, 1)
        used = (lane < BLOCK) | full
        codes = jnp.where(used, jnp.maximum(pre_act, 0.0), 0.0).astype(BF16)
        total[...] += jnp.dot(codes, dec_kept[pair], preferred_element_type=F32)
        return carry

    lax.fori_loop(0, pairs, step, 0)
    rows = keep_ref.shape[0]
    core = lax.rem(where, 2)
    keep_ref[...] = total[pl.ds(pl.multiple_of(core * rows, rows), rows), :]
    send_ref[...] = total[pl.ds(pl.multiple_of((1 - core) * rows, rows), rows), :].astype(BF16)


def code_gradient(ids_ref, own_ref, other_ref, dec_kept, out_ref, grad):
    blocks = out_ref.shape[1] // BLOCK
    rows = own_ref.shape[0]
    core = lax.rem(lax.axis_index("latent"), 2)
    grad[pl.ds(pl.multiple_of(core * rows, rows), rows), :] = own_ref[...]
    grad[pl.ds(pl.multiple_of((1 - core) * rows, rows), rows), :] = other_ref[...]
    out_ref[...] = jnp.zeros_like(out_ref)
    live_count = ids_ref[0, blocks]

    def step(pair, carry):
        n = 2 * pair
        product = lax.dot_general(
            grad[...], dec_kept[pair], (((1,), (1,)), ((), ())), preferred_element_type=F32
        ).astype(BF16)
        out_ref[:, pl.ds(pl.multiple_of(ids_ref[0, n] * BLOCK, BLOCK), BLOCK)] = product[:, :BLOCK]

        @pl.when(n + 1 < live_count)
        def _():
            out_ref[:, pl.ds(pl.multiple_of(ids_ref[0, n + 1] * BLOCK, BLOCK), BLOCK)] = product[:, BLOCK:]

        return carry

    lax.fori_loop(0, lax.div(live_count + 1, 2), step, 0)


def swap(value, axis, bit):
    size = lax.axis_size(axis)
    return lax.ppermute(value, axis, [(i, i ^ bit) for i in range(size)])


def swap_both(value, layer_bit, latent_bit):
    layers, latents = lax.axis_size("layer"), lax.axis_size("latent")
    pairs = [
        (l * latents + k, (l ^ layer_bit) * latents + (k ^ latent_bit)) for l in range(layers) for k in range(latents)
    ]
    return lax.ppermute(value, ("layer", "latent"), pairs)


def part(value, start, size, axis):
    return lax.dynamic_slice_in_dim(value, start, size, axis)


def local(residuals, targets, enc_weight, enc_bias, dec_weight, out_gain, block_list, block_count):
    tok_rows, model_width = residuals.shape[1:]
    local_latents = enc_weight.shape[2]
    blocks = local_latents // BLOCK
    pair_slots = (blocks + 1) // 2
    layers, latents = lax.axis_size("layer"), lax.axis_size("latent")
    layer, latent = lax.axis_index("layer"), lax.axis_index("latent")
    core = latent % 2
    rows = tok_rows // 2
    chips = latents // 2
    width = model_width // chips
    column = (latent // 2) * width

    gain = part(out_gain, column, width, 1)
    target = part(part(targets[0], core * rows, rows, 0), column, width, 1)
    square = gain * gain
    layer_bits = [1 << s for s in range((layers - 1).bit_length())]
    near_gain = swap(gain, "layer", 1)
    near_target = swap(target, "layer", 1)
    chip_bits = [1 << s for s in range((chips - 1).bit_length(), 0, -1)]

    vmem = pl.BlockSpec(memory_space=pltpu.VMEM)
    smem = pl.BlockSpec(memory_space=pltpu.SMEM)
    anyw = pl.BlockSpec(memory_space=pl.ANY)
    keep, send, dec_kept, ids = pl.pallas_call(
        encode_decode,
        out_shape=(
            jax.ShapeDtypeStruct((rows, model_width), F32),
            jax.ShapeDtypeStruct((rows, model_width), BF16),
            pltpu.VMEM((pair_slots, PAIR, model_width), BF16),
            jax.ShapeDtypeStruct((1, blocks + 1), jnp.int32),
        ),
        in_specs=[smem, smem, vmem, vmem, anyw, anyw],
        out_specs=(vmem, vmem, vmem, smem),
        scratch_shapes=[
            pltpu.VMEM((pair_slots, model_width, PAIR), BF16),
            pltpu.VMEM((tok_rows, model_width), F32),
            pltpu.SemaphoreType.DMA((blocks,)),
            pltpu.SemaphoreType.DMA((blocks,)),
        ],
        compiler_params=pltpu.CompilerParams(vmem_limit_bytes=48 << 20),
        name="encode_decode",
    )(block_list, block_count, residuals[0], enc_bias, enc_weight[0], dec_weight[0])

    held = keep + swap(send, "latent", 1).astype(F32)
    for bit in chip_bits[:-1]:
        half = held.shape[1] // 2
        upper = (latent & bit) != 0
        away = jnp.where(upper, held[:, :half], held[:, half:]).astype(BF16)
        mine = jnp.where(upper, held[:, half:], held[:, :half])
        held = mine + swap(away, "latent", bit).astype(F32)
    bit = chip_bits[-1]
    half = held.shape[1] // 2
    upper = (latent & bit) != 0
    away = jnp.where(upper, held[:, :half], held[:, half:]).astype(BF16)
    mine = jnp.where(upper, held[:, half:], held[:, :half])
    from_near = swap(mine.astype(BF16), "layer", 1)
    from_chip = swap(away, "latent", bit)
    from_both = swap_both(away, 1, bit)
    own = mine + from_chip.astype(F32)
    near = from_near.astype(F32) + from_both.astype(F32)

    low = (layer & 1) == 0
    near_square = near_gain * near_gain
    own_error = square * own - gain * target.astype(F32)
    near_error = near_square * near - near_gain * near_target.astype(F32)
    before = jnp.where(low, own, own + near)
    after = jnp.where(low, own_error + near_square * own + near_error, own_error + square * near)
    after_square = jnp.where(low, square + near_square, square)
    all_before = own + near
    all_after = own_error + near_error + jnp.where(low, near_square * own, square * near)
    all_square = square + near_square
    for step in layer_bits[1:]:
        low = (layer & step) == 0
        there_square = swap(all_square, "layer", step)
        if step == layer_bits[-1]:
            got = swap(jnp.where(low, all_before, all_after).astype(BF16), "layer", step).astype(F32)
            there_before = there_after = got
        else:
            there_before = swap(all_before.astype(BF16), "layer", step).astype(F32)
            there_after = swap(all_after.astype(BF16), "layer", step).astype(F32)
        before, after = (
            jnp.where(low, before, before + there_before),
            jnp.where(low, after + there_square * all_before + there_after, after + after_square * there_before),
        )
        after_square = jnp.where(low, after_square + there_square, after_square)
        all_before, all_after = (
            all_before + there_before,
            all_after + there_after + jnp.where(low, there_square * all_before, all_square * there_before),
        )
        all_square = all_square + there_square

    grad_in = after.astype(BF16)
    fitted = gain * before
    error_term = fitted - target.astype(F32)
    loss = jnp.sum(error_term * error_term).reshape(1, 1)

    for bit in reversed(chip_bits):
        upper = (latent & bit) != 0
        got = swap(grad_in, "latent", bit)
        grad_in = jnp.concatenate([jnp.where(upper, got, grad_in), jnp.where(upper, grad_in, got)], axis=1)
        loss = loss + swap(loss, "latent", bit)
    other_rows = swap(grad_in, "latent", 1)
    loss = (loss + swap(loss, "latent", 1)) / (tok_rows * model_width)

    recon = fitted.astype(BF16)
    columns = width // 2
    stay = part(recon, core * columns, columns, 1)
    got = swap(part(recon, (1 - core) * columns, columns, 1), "latent", 1)
    recon = jnp.concatenate([jnp.where(core == 0, stay, got), jnp.where(core == 0, got, stay)], axis=0)

    code_grad = pl.pallas_call(
        code_gradient,
        out_shape=jax.ShapeDtypeStruct((tok_rows, local_latents), BF16),
        in_specs=[smem, vmem, vmem, vmem],
        out_specs=vmem,
        scratch_shapes=[pltpu.VMEM((tok_rows, model_width), BF16)],
        compiler_params=pltpu.CompilerParams(vmem_limit_bytes=24 << 20),
        name="code_gradient",
    )(ids, grad_in, other_rows, pltpu.with_memory_space_constraint(dec_kept, pltpu.VMEM))
    return recon[None], code_grad[None], loss


def solution(mesh):
    placed = (
        P("layer", "groups", None),
        P("layer", "groups", None),
        P("layer", None, "latent"),
        P("layer", "latent"),
        P("layer", "latent", None),
        P("layer", None),
        P("layer", "groups", None),
        P("layer", "groups"),
    )
    return jax.shard_map(
        local,
        mesh=mesh,
        in_specs=placed,
        out_specs=(
            P("layer", "groups", "latent"),
            P("layer", "groups", "latent"),
            P("groups", "layer"),
        ),
        check_vma=False,
    )
```

time: 272 us -> 57.7 us (0.21)
  the two profiles are of different devices: /device:TPU:0 before, /device:TPU:1 now
where the time goes in v1:
time: 57.7 us; the launch traced here: 57.8 us
  waiting for transfers between devices  16.9 us (29%)
  starting transfers between devices  13.9 us (24%)
  Pallas kernels  11.1 us (19%)
  local copies, waits for them, and re-layouts  8.88 us (15%)
  between operations  4.44 us (8%)
  other arithmetic  2.69 us (5%)
    ppermute x12, waiting for transfers between devices, swap(): return lax.ppermute(value, axis, [(i, i ^ bit) for i in range(size)])  12.4 us
    ppermute x12, starting transfers between devices, swap(): return lax.ppermute(value, axis, [(i, i ^ bit) for i in range(size)])  10.5 us
    unnamed x11, local copies, waits for them, and re-layouts  8.67 us
    pallas_call x1, Pallas kernels, local(): pl.pallas_call(encode_decode, out_shape=(jax.ShapeDtypeStruct((rows, mode...  7.49 us
    ppermute x1, waiting for transfers between devices, swap_both(): return lax.ppermute(value, ('layer', 'latent'), pairs)  4.53 us
    pallas_call x1, Pallas kernels, local(): pl.pallas_call(code_gradient, out_shape=jax.ShapeDtypeStruct((tok_rows, l...  3.59 us
    ppermute x1, starting transfers between devices, swap_both(): return lax.ppermute(value, ('layer', 'latent'), pairs)  3.38 us
  transfers between devices with their start and end apart: 13, of which 7 were waited for; matrix products, arithmetic and copies ran while one was open for 4% of the time, Pallas kernels for 0%

profile of v1, /device:TPU:1, one launch (start us, length us, event | category | flops | bytes accessed | tf_op | source)
XLA Modules:
  0.0 57.8 jit_solution(7239720180345196855)
XLA Ops:
  1.3 7.5 %encode_decode.1 = (f32[64,2304]{1,0:T(8,128)}, bf16[64,2304]{1,0:T(8,128)(2,1)}, bf16[8,256,2304]{2,1,0:T(8,128)(2,1)S(1)}, s32[1,17]{1,0:T(1,128)}) custom-call(s32[1,1,24]{2,1,0:T(1,128)} %list_ref.1, s32[1,1]{1,0:T(1,128)S(6)} %copy.12.count_ref, bf16[128,2304]{1,0:T(8,128)(2,1)} %bitcast.15, f32[1,2048]{1,0:T(1,128)} %bias_ref.1, ...), custom_call_target="tpu_custom_call" | custom-call | tf_op jit(solution)/shard_map/encode_decode/pallas_call | solution.py:150
  8.8 3.6 %copy-done = bf16[8,256,2304]{2,1,0:T(8,128)(2,1)} copy-done((bf16[8,256,2304]{2,1,0:T(8,128)(2,1)}, bf16[8,256,2304]{2,1,0:T(8,128)(2,1)S(1)}, u32[]{:S(2)}) %copy-start) | copy-done | bytes 9437208
  12.6 1.2 %collective-permute-start.5 = (bf16[64,1152]{1,0:T(8,128)(2,1)S(1)}, bf16[64,1152]{1,0:T(8,128)(2,1)S(1)}, u32[]{:S(2)}, u32[]{:S(2)}) collective-permute-start(bf16[64,1152]{1,0:T(8,128)(2,1)S(1)} %dynamic-slice_bitcast_fusion), channel_id=1, source_target_pairs={{0,4},{4,0},{8,12},{12,8},{1,5},{5,1},{9,13},{13,9},{2,6},{6,2},{1... | collective-permute-start | bytes 442376 | tf_op jit(solution)/shard_map/ppermute | solution.py:111
  13.8 0.3 collective-permute-start.4
  14.2 1.1 %convert_add_fusion = f32[64,2304]{1,0:T(8,128)S(1)} fusion(f32[64,2304]{1,0:T(8,128)} %get-tuple-element.7, bf16[64,2304]{1,0:T(8,128)(2,1)S(1)} %collective-permute-done), kind=kLoop, calls=%fused_computation | loop fusion | flops 294912 | bytes 1474560 | tf_op jit(solution)/shard_map/add | solution.py:170
  15.4 3.4 %collective-permute-start.3 = (bf16[64,1152]{1,0:T(8,128)(2,1)S(1)}, bf16[64,1152]{1,0:T(8,128)(2,1)S(1)}, u32[]{:S(2)}, u32[]{:S(2)}) collective-permute-start(bf16[64,1152]{1,0:T(8,128)(2,1)S(1)} %select_convert_fusion.1), channel_id=1, source_target_pairs={{0,6},{1,7},{2,4},{3,5},{4,2},{5,3},{6,0},{7,1},{8,14},{9,15},{10,... | collective-permute-start | bytes 442376 | tf_op jit(solution)/shard_map/ppermute | solution.py:119
  19.1 1.1 %collective-permute-start.2 = (bf16[64,1152]{1,0:T(8,128)(2,1)S(1)}, bf16[64,1152]{1,0:T(8,128)(2,1)S(1)}, u32[]{:S(2)}, u32[]{:S(2)}) collective-permute-start(bf16[64,1152]{1,0:T(8,128)(2,1)S(1)} %get-tuple-element.21), channel_id=1, source_target_pairs={{0,4},{4,0},{8,12},{12,8},{1,5},{5,1},{9,13},{13,9},{2,6},{6,2},{1... | collective-permute-start | bytes 442376 | tf_op jit(solution)/shard_map/ppermute | solution.py:111
  20.3 4.5 %collective-permute-done.3 = bf16[64,1152]{1,0:T(8,128)(2,1)S(1)} collective-permute-done((bf16[64,1152]{1,0:T(8,128)(2,1)S(1)}, bf16[64,1152]{1,0:T(8,128)(2,1)S(1)}, u32[]{:S(2)}, u32[]{:S(2)}) %collective-permute-start.3) | collective-permute-done | bytes 147488 | tf_op jit(solution)/shard_map/ppermute | solution.py:119
  24.8 2.0 %collective-permute-done.2 = bf16[64,1152]{1,0:T(8,128)(2,1)S(1)} collective-permute-done((bf16[64,1152]{1,0:T(8,128)(2,1)S(1)}, bf16[64,1152]{1,0:T(8,128)(2,1)S(1)}, u32[]{:S(2)}, u32[]{:S(2)}) %collective-permute-start.2) | collective-permute-done | bytes 147488 | tf_op jit(solution)/shard_map/ppermute | solution.py:111
  26.8 0.4 collective-permute-done.1
  27.5 2.2 %collective-permute-start.6 = (bf16[64,1152]{1,0:T(8,128)(2,1)S(1)}, bf16[64,1152]{1,0:T(8,128)(2,1)S(1)}, u32[]{:S(2)}, u32[]{:S(2)}) collective-permute-start(bf16[64,1152]{1,0:T(8,128)(2,1)S(1)} %select_convert_fusion), channel_id=1, source_target_pairs={{0,8},{4,12},{8,0},{12,4},{1,9},{5,13},{9,1},{13,5},{2,10},{6,14},... | collective-permute-start | bytes 442376 | tf_op jit(solution)/shard_map/ppermute | solution.py:111
  30.0 7.0 %collective-permute-done.8 = f32[1,1152]{1,0:T(1,128)S(1)} collective-permute-done((f32[1,1152]{1,0:T(1,128)S(1)}, f32[1,1152]{1,0:T(1,128)S(1)}, u32[]{:S(2)}, u32[]{:S(2)}) %collective-permute-start.8) | collective-permute-done | bytes 4640 | tf_op jit(solution)/shard_map/ppermute | solution.py:111
  37.0 1.0 %fusion.2 = (f32[]{:T(128)}, bf16[64,1152]{1,0:T(8,128)(2,1)S(1)}, bf16[64,1152]{1,0:T(8,128)(2,1)S(1)}) fusion(bf16[64,1152]{1,0:T(8,128)(2,1)S(1)} %collective-permute-done.6, bf16[64,1152]{1,0:T(8,128)(2,1)S(1)} %collective-permute-done.3, bf16[64,1152]{1,0:T(8,128)(2,1)S(1)} %collective-permute-done.2, f32[64,1152]{1,0:T(8,128)S(1)} %get-tuple-element.22, ...), kind=kLoop, calls=%fused_computation.8 | loop fusion | flops 2654207 | bytes 1502222 | tf_op jit(solution)/shard_map/reduce_sum | solution.py:221
  38.0 1.2 %collective-permute-start.9 = (bf16[64,1152]{1,0:T(8,128)(2,1)S(1)}, bf16[64,1152]{1,0:T(8,128)(2,1)S(1)}, u32[]{:S(2)}, u32[]{:S(2)}) collective-permute-start(bf16[64,1152]{1,0:T(8,128)(2,1)S(1)} %get-tuple-element.23), channel_id=1, source_target_pairs={{0,2},{1,3},{2,0},{3,1},{4,6},{5,7},{6,4},{7,5},{8,10},{9,11},{10,... | collective-permute-start | bytes 442376 | tf_op jit(solution)/shard_map/ppermute | solution.py:111
  39.3 1.3 %collective-permute-start.7 = (bf16[64,576]{1,0:T(8,128)(2,1)S(1)}, bf16[64,576]{1,0:T(8,128)(2,1)S(1)}, u32[]{:S(2)}, u32[]{:S(2)}) collective-permute-start(bf16[64,576]{1,0:T(8,128)(2,1)S(1)} %constant_dynamic-slice_fusion), channel_id=1, source_target_pairs={{0,1},{1,0},{2,3},{3,2},{4,5},{5,4},{6,7},{7,6},{8,9},{9,8},{10,11... | collective-permute-start | bytes 221192 | tf_op jit(solution)/shard_map/ppermute | solution.py:111
  40.6 0.5 collective-permute-start.11
  41.1 2.3 %collective-permute-done.11 = f32[1,1]{1,0:T(1,128)} collective-permute-done((f32[1,1]{1,0:T(1,128)}, f32[1,1]{1,0:T(1,128)}, u32[]{:S(2)}, u32[]{:S(2)}) %collective-permute-start.11) | collective-permute-done | bytes 36 | tf_op jit(solution)/shard_map/ppermute | solution.py:111
  44.7 1.8 %collective-permute-start.12 = (f32[1,1]{1,0:T(1,128)}, f32[1,1]{1,0:T(1,128)}, u32[]{:S(2)}, u32[]{:S(2)}) collective-permute-start(f32[1,1]{1,0:T(1,128)} %add.90), channel_id=1, source_target_pairs={{0,1},{1,0},{2,3},{3,2},{4,5},{5,4},{6,7},{7,6},{8,9},{9,8},{10,11... | collective-permute-start | bytes 20 | tf_op jit(solution)/shard_map/ppermute | solution.py:111
  47.2 0.3 collective-permute-start.10
  47.7 0.8 %copy.11 = bf16[1,128,576]{1,2,0:T(8,128)(2,1)} copy(bf16[1,128,576]{2,1,0:T(8,128)(2,1)S(1)} %maximum_bitcast_fusion) | data formatting | bytes 294912
  48.5 0.4 collective-permute-done.10.other_ref
  48.9 3.7 %copy-done.1 = bf16[8,256,2304]{2,1,0:T(8,128)(2,1)S(1)} copy-done((bf16[8,256,2304]{2,1,0:T(8,128)(2,1)S(1)}, bf16[8,256,2304]{2,1,0:T(8,128)(2,1)}, u32[]{:S(2)}) %copy-start.1) | copy-done | bytes 9437208
  52.6 0.6 copy-done.2
  53.1 3.6 %code_gradient.1 = bf16[128,2048]{1,0:T(8,128)(2,1)} custom-call(s32[1,17]{1,0:T(1,128)S(1)} %copy-done.2, bf16[64,2304]{1,0:T(8,128)(2,1)S(1)} %pad_maximum_fusion.own_ref, bf16[64,2304]{1,0:T(8,128)(2,1)S(1)} %collective-permute-done.10.other_ref, bf16[8,256,2304]{2,1,0:T(8,128)(2,1)S(1)} %copy-done.1), custom_call_target="tpu_custom_call" | custom-call | tf_op jit(solution)/shard_map/code_gradient/pallas_call | solution.py:237
  (29 shorter events, 1.4 us)
Async XLA Ops:
  1.3 11.1 %copy-start.3 = (bf16[1,128,2304]{2,1,0:T(8,128)(2,1)S(1)}, bf16[1,128,2304]{2,1,0:T(8,128)(2,1)}, u32[]{:S(2)}) copy-start(bf16[1,128,2304]{2,1,0:T(8,128)(2,1)} %param.9) | copy-start | bytes 1769476
  1.3 12.5 %copy-start.4 = (f32[1,2304]{1,0:T(1,128)S(1)}, f32[1,2304]{1,0:T(1,128)}, u32[]{:S(2)}) copy-start(f32[1,2304]{1,0:T(1,128)} %param.13) | copy-start | bytes 27652
  8.8 3.6 %copy-start = (bf16[8,256,2304]{2,1,0:T(8,128)(2,1)}, bf16[8,256,2304]{2,1,0:T(8,128)(2,1)S(1)}, u32[]{:S(2)}) copy-start(bf16[8,256,2304]{2,1,0:T(8,128)(2,1)S(1)} %get-tuple-element.10.dec_kept) | copy-start | bytes 28311556
  12.4 1.8 %collective-permute-start = (bf16[64,2304]{1,0:T(8,128)(2,1)}, bf16[64,2304]{1,0:T(8,128)(2,1)S(1)}, u32[]{:S(2)}, u32[]{:S(2)}) collective-permute-start(bf16[64,2304]{1,0:T(8,128)(2,1)} %get-tuple-element.8), channel_id=1, source_target_pairs={{0,1},{1,0},{2,3},{3,2},{4,5},{5,4},{6,7},{7,6},{8,9},{9,8},{10,11... | collective-permute-start | bytes 884744 | tf_op jit(solution)/shard_map/ppermute | solution.py:111
  12.6 7.7 %collective-permute-start.5 = (bf16[64,1152]{1,0:T(8,128)(2,1)S(1)}, bf16[64,1152]{1,0:T(8,128)(2,1)S(1)}, u32[]{:S(2)}, u32[]{:S(2)}) collective-permute-start(bf16[64,1152]{1,0:T(8,128)(2,1)S(1)} %dynamic-slice_bitcast_fusion), channel_id=1, source_target_pairs={{0,4},{4,0},{8,12},{12,8},{1,5},{5,1},{9,13},{13,9},{2,6},{6,2},{1... | collective-permute-start | bytes 442376 | tf_op jit(solution)/shard_map/ppermute | solution.py:111
  13.8 6.4 %collective-permute-start.4 = (f32[1,1152]{1,0:T(1,128)S(1)}, f32[1,1152]{1,0:T(1,128)S(1)}, u32[]{:S(2)}, u32[]{:S(2)}) collective-permute-start(f32[1,1152]{1,0:T(1,128)S(1)} %constant_dynamic-slice_fusion.1), channel_id=1, source_target_pairs={{0,4},{4,0},{8,12},{12,8},{1,5},{5,1},{9,13},{13,9},{2,6},{6,2},{1... | collective-permute-start | bytes 13832 | tf_op jit(solution)/shard_map/ppermute | solution.py:111
  15.4 9.4 %collective-permute-start.3 = (bf16[64,1152]{1,0:T(8,128)(2,1)S(1)}, bf16[64,1152]{1,0:T(8,128)(2,1)S(1)}, u32[]{:S(2)}, u32[]{:S(2)}) collective-permute-start(bf16[64,1152]{1,0:T(8,128)(2,1)S(1)} %select_convert_fusion.1), channel_id=1, source_target_pairs={{0,6},{1,7},{2,4},{3,5},{4,2},{5,3},{6,0},{7,1},{8,14},{9,15},{10,... | collective-permute-start | bytes 442376 | tf_op jit(solution)/shard_map/ppermute | solution.py:119
  18.8 8.5 %collective-permute-start.1 = (bf16[64,1152]{1,0:T(8,128)(2,1)S(1)}, bf16[64,1152]{1,0:T(8,128)(2,1)S(1)}, u32[]{:S(2)}, u32[]{:S(2)}) collective-permute-start(bf16[64,1152]{1,0:T(8,128)(2,1)S(1)} %select_convert_fusion.1), channel_id=1, source_target_pairs={{0,2},{1,3},{2,0},{3,1},{4,6},{5,7},{6,4},{7,5},{8,10},{9,11},{10,... | collective-permute-start | bytes 442376 | tf_op jit(solution)/shard_map/ppermute | solution.py:111
  19.1 7.8 %collective-permute-start.2 = (bf16[64,1152]{1,0:T(8,128)(2,1)S(1)}, bf16[64,1152]{1,0:T(8,128)(2,1)S(1)}, u32[]{:S(2)}, u32[]{:S(2)}) collective-permute-start(bf16[64,1152]{1,0:T(8,128)(2,1)S(1)} %get-tuple-element.21), channel_id=1, source_target_pairs={{0,4},{4,0},{8,12},{12,8},{1,5},{5,1},{9,13},{13,9},{2,6},{6,2},{1... | collective-permute-start | bytes 442376 | tf_op jit(solution)/shard_map/ppermute | solution.py:111
  27.5 9.5 %collective-permute-start.6 = (bf16[64,1152]{1,0:T(8,128)(2,1)S(1)}, bf16[64,1152]{1,0:T(8,128)(2,1)S(1)}, u32[]{:S(2)}, u32[]{:S(2)}) collective-permute-start(bf16[64,1152]{1,0:T(8,128)(2,1)S(1)} %select_convert_fusion), channel_id=1, source_target_pairs={{0,8},{4,12},{8,0},{12,4},{1,9},{5,13},{9,1},{13,5},{2,10},{6,14},... | collective-permute-start | bytes 442376 | tf_op jit(solution)/shard_map/ppermute | solution.py:111
  29.8 7.2 %collective-permute-start.8 = (f32[1,1152]{1,0:T(1,128)S(1)}, f32[1,1152]{1,0:T(1,128)S(1)}, u32[]{:S(2)}, u32[]{:S(2)}) collective-permute-start(f32[1,1152]{1,0:T(1,128)S(1)} %get-tuple-element.28), channel_id=1, source_target_pairs={{0,8},{4,12},{8,0},{12,4},{1,9},{5,13},{9,1},{13,5},{2,10},{6,14},... | collective-permute-start | bytes 13832 | tf_op jit(solution)/shard_map/ppermute | solution.py:111
  38.0 9.1 %collective-permute-start.9 = (bf16[64,1152]{1,0:T(8,128)(2,1)S(1)}, bf16[64,1152]{1,0:T(8,128)(2,1)S(1)}, u32[]{:S(2)}, u32[]{:S(2)}) collective-permute-start(bf16[64,1152]{1,0:T(8,128)(2,1)S(1)} %get-tuple-element.23), channel_id=1, source_target_pairs={{0,2},{1,3},{2,0},{3,1},{4,6},{5,7},{6,4},{7,5},{8,10},{9,11},{10,... | collective-permute-start | bytes 442376 | tf_op jit(solution)/shard_map/ppermute | solution.py:111
  39.3 8.3 %collective-permute-start.7 = (bf16[64,576]{1,0:T(8,128)(2,1)S(1)}, bf16[64,576]{1,0:T(8,128)(2,1)S(1)}, u32[]{:S(2)}, u32[]{:S(2)}) collective-permute-start(bf16[64,576]{1,0:T(8,128)(2,1)S(1)} %constant_dynamic-slice_fusion), channel_id=1, source_target_pairs={{0,1},{1,0},{2,3},{3,2},{4,5},{5,4},{6,7},{7,6},{8,9},{9,8},{10,11... | collective-permute-start | bytes 221192 | tf_op jit(solution)/shard_map/ppermute | solution.py:111
  40.6 2.8 %collective-permute-start.11 = (f32[1,1]{1,0:T(1,128)}, f32[1,1]{1,0:T(1,128)}, u32[]{:S(2)}, u32[]{:S(2)}) collective-permute-start(f32[1,1]{1,0:T(1,128)} %bitcast.6), channel_id=1, source_target_pairs={{0,2},{1,3},{2,0},{3,1},{4,6},{5,7},{6,4},{7,5},{8,10},{9,11},{10,... | collective-permute-start | bytes 20 | tf_op jit(solution)/shard_map/ppermute | solution.py:111
  44.7 1.8 %collective-permute-start.12 = (f32[1,1]{1,0:T(1,128)}, f32[1,1]{1,0:T(1,128)}, u32[]{:S(2)}, u32[]{:S(2)}) collective-permute-start(f32[1,1]{1,0:T(1,128)} %add.90), channel_id=1, source_target_pairs={{0,1},{1,0},{2,3},{3,2},{4,5},{5,4},{6,7},{7,6},{8,9},{9,8},{10,11... | collective-permute-start | bytes 20 | tf_op jit(solution)/shard_map/ppermute | solution.py:111
  47.2 1.6 %collective-permute-start.10 = (bf16[64,2304]{1,0:T(8,128)(2,1)S(1)}, bf16[64,2304]{1,0:T(8,128)(2,1)S(1)}, u32[]{:S(2)}, u32[]{:S(2)}) collective-permute-start(bf16[64,2304]{1,0:T(8,128)(2,1)S(1)} %pad_maximum_fusion.own_ref), channel_id=1, source_target_pairs={{0,1},{1,0},{2,3},{3,2},{4,5},{5,4},{6,7},{7,6},{8,9},{9,8},{10,11... | collective-permute-start | bytes 884744 | tf_op jit(solution)/shard_map/ppermute | solution.py:111
  48.9 3.7 %copy-start.1 = (bf16[8,256,2304]{2,1,0:T(8,128)(2,1)S(1)}, bf16[8,256,2304]{2,1,0:T(8,128)(2,1)}, u32[]{:S(2)}) copy-start(bf16[8,256,2304]{2,1,0:T(8,128)(2,1)} %copy-done) | copy-start | bytes 28311556
  52.5 0.6 copy-start.2

commit v2 on v1

--- a/solution.py
+++ b/solution.py
@@ -9,24 +9,42 @@
 
 BLOCK = 128
 PAIR = 2 * BLOCK
+KEPT_PAIRS = 1
 F32 = jnp.float32
 BF16 = jnp.bfloat16
 
 
-def encode_decode(list_ref, count_ref, x_ref, bias_ref, enc_ref, dec_ref, keep_ref, send_ref, dec_kept, ids_ref, enc_held, total, enc_sem, dec_sem):
+def dec_copy(dec_ref, dec_kept, dec_more, sem, block, n, start):
+    kept = dec_kept.shape[0]
+    pair, half = lax.div(n, 2), pl.multiple_of(lax.rem(n, 2) * BLOCK, BLOCK)
+    source = dec_ref.at[pl.ds(pl.multiple_of(block * BLOCK, BLOCK), BLOCK), :]
+
+    def move(held, slot):
+        copy = pltpu.make_async_copy(source, held.at[slot, pl.ds(half, BLOCK), :], sem.at[n])
+        copy.start() if start else copy.wait()
+
+    pl.when(pair < kept)(lambda: move(dec_kept, pair))
+    pl.when(pair >= kept)(lambda: move(dec_more, pair - kept))
+
+
+def encode_decode(list_ref, count_ref, x_any, bias_any, enc_ref, dec_ref, keep_ref, send_ref, dec_kept, ids_ref, x_ref, bias_ref, dec_more, enc_held, total, in_sem, enc_sem, dec_sem):
+    loads = [pltpu.make_async_copy(x_any, x_ref, in_sem.at[0]), pltpu.make_async_copy(bias_any, bias_ref, in_sem.at[1])]
+    for load in loads:
+        load.start()
     blocks = enc_ref.shape[1] // BLOCK
     where = lax.axis_index("latent")
     first = where * blocks
     slots = list_ref.shape[2]
     count = count_ref[0, 0]
 
-    def copies(block, n):
-        pair, half = lax.div(n, 2), lax.rem(n, 2) * BLOCK
-        half = pl.multiple_of(half, BLOCK)
-        start = pl.multiple_of(block * BLOCK, BLOCK)
-        return (
-            pltpu.make_async_copy(enc_ref.at[:, pl.ds(start, BLOCK)], enc_held.at[pair, :, pl.ds(half, BLOCK)], enc_sem.at[n]),
-            pltpu.make_async_copy(dec_ref.at[pl.ds(start, BLOCK), :], dec_kept.at[pair, pl.ds(half, BLOCK), :], dec_sem.at[n]),
+    kept = dec_kept.shape[0]
+
+    def enc_copy(block, n):
+        half = pl.multiple_of(lax.rem(n, 2) * BLOCK, BLOCK)
+        return pltpu.make_async_copy(
+            enc_ref.at[:, pl.ds(pl.multiple_of(block * BLOCK, BLOCK), BLOCK)],
+            enc_held.at[lax.div(n, 2), :, pl.ds(half, BLOCK)],
+            enc_sem.at[n],
         )
 
     def look(slot, n):
@@ -36,8 +54,8 @@
         @pl.when(live)
         def _():
             ids_ref[0, n] = block
-            for copy in copies(block, n):
-                copy.start()
+            enc_copy(block, n).start()
+            dec_copy(dec_ref, dec_kept, dec_more, dec_sem, block, n, True)
 
         return n + live.astype(jnp.int32)
 
@@ -49,20 +67,32 @@
 
     @pl.when(odd)
     def _():
-        dec_kept[pairs - 1, pl.ds(BLOCK, BLOCK), :] = jnp.zeros((BLOCK, dec_kept.shape[2]), BF16)
+        zeros = jnp.zeros((BLOCK, dec_kept.shape[2]), BF16)
+
+        @pl.when(pairs <= kept)
+        def _():
+            dec_kept[pairs - 1, pl.ds(BLOCK, BLOCK), :] = zeros
+
+        @pl.when(pairs > kept)
+        def _():
+            dec_more[pairs - 1 - kept, pl.ds(BLOCK, BLOCK), :] = zeros
+
         ids_ref[0, live_count] = ids_ref[0, live_count - 1]
 
-    def step(pair, carry):
+    for load in loads:
+        load.wait()
+
+    def step(held, offset, pair, carry):
         n = 2 * pair
         full = n + 1 < live_count
         one, two = ids_ref[0, n], ids_ref[0, n + 1]
-        for copy in copies(one, n):
-            copy.wait()
+        enc_copy(one, n).wait()
+        dec_copy(dec_ref, dec_kept, dec_more, dec_sem, one, n, False)
 
         @pl.when(full)
         def _():
-            for copy in copies(two, n + 1):
-                copy.wait()
+            enc_copy(two, n + 1).wait()
+            dec_copy(dec_ref, dec_kept, dec_more, dec_sem, two, n + 1, False)
 
         bias = jnp.concatenate(
             [bias_ref[:, pl.ds(pl.multiple_of(block * BLOCK, BLOCK), BLOCK)] for block in (one, two)], axis=1
@@ -71,39 +101,60 @@
         lane = lax.broadcasted_iota(jnp.int32, pre_act.shape, 1)
         used = (lane < BLOCK) | full
         codes = jnp.where(used, jnp.maximum(pre_act, 0.0), 0.0).astype(BF16)
-        total[...] += jnp.dot(codes, dec_kept[pair], preferred_element_type=F32)
+        total[...] += jnp.dot(codes, held[pair - offset], preferred_element_type=F32)
         return carry
 
-    lax.fori_loop(0, pairs, step, 0)
+    lax.fori_loop(0, jnp.minimum(pairs, kept), functools.partial(step, dec_kept, 0), 0)
+    lax.fori_loop(kept, pairs, functools.partial(step, dec_more, kept), 0)
     rows = keep_ref.shape[0]
     core = lax.rem(where, 2)
     keep_ref[...] = total[pl.ds(pl.multiple_of(core * rows, rows), rows), :]
     send_ref[...] = total[pl.ds(pl.multiple_of((1 - core) * rows, rows), rows), :].astype(BF16)
 
 
-def code_gradient(ids_ref, own_ref, other_ref, dec_kept, out_ref, grad):
+def code_gradient(ids_ref, own_ref, other_ref, loss_ref, chip_loss_ref, dec_kept, dec_ref, out_ref, mean_ref, grad, dec_more, dec_sem):
     blocks = out_ref.shape[1] // BLOCK
+    kept = dec_kept.shape[0]
     rows = own_ref.shape[0]
+    live_count = ids_ref[0, blocks]
+
+    def fetch(n, carry):
+        dec_copy(dec_ref, dec_kept, dec_more, dec_sem, ids_ref[0, n], n, True)
+        return carry
+
+    lax.fori_loop(2 * kept, live_count, fetch, 0)
     core = lax.rem(lax.axis_index("latent"), 2)
     grad[pl.ds(pl.multiple_of(core * rows, rows), rows), :] = own_ref[...]
     grad[pl.ds(pl.multiple_of((1 - core) * rows, rows), rows), :] = other_ref[...]
     out_ref[...] = jnp.zeros_like(out_ref)
-    live_count = ids_ref[0, blocks]
-
-    def step(pair, carry):
+    both = loss_ref[...] + chip_loss_ref[...]
+    mean_ref[...] = jnp.sum(both, axis=1, keepdims=True) / (2 * rows * own_ref.shape[1])
+
+    def step(held, offset, pair, carry):
         n = 2 * pair
+        full = n + 1 < live_count
+
+        if offset:
+            dec_copy(dec_ref, dec_kept, dec_more, dec_sem, ids_ref[0, n], n, False)
+
+            @pl.when(full)
+            def _():
+                dec_copy(dec_ref, dec_kept, dec_more, dec_sem, ids_ref[0, n + 1], n + 1, False)
+
         product = lax.dot_general(
-            grad[...], dec_kept[pair], (((1,), (1,)), ((), ())), preferred_element_type=F32
+            grad[...], held[pair - offset], (((1,), (1,)), ((), ())), preferred_element_type=F32
         ).astype(BF16)
         out_ref[:, pl.ds(pl.multiple_of(ids_ref[0, n] * BLOCK, BLOCK), BLOCK)] = product[:, :BLOCK]
 
-        @pl.when(n + 1 < live_count)
+        @pl.when(full)
         def _():
             out_ref[:, pl.ds(pl.multiple_of(ids_ref[0, n + 1] * BLOCK, BLOCK), BLOCK)] = product[:, BLOCK:]
 
         return carry
 
-    lax.fori_loop(0, lax.div(live_count + 1, 2), step, 0)
+    pairs = lax.div(live_count + 1, 2)
+    lax.fori_loop(0, jnp.minimum(pairs, kept), functools.partial(step, dec_kept, 0), 0)
+    lax.fori_loop(kept, pairs, functools.partial(step, dec_more, kept), 0)
 
 
 def swap(value, axis, bit):
@@ -128,6 +179,8 @@
     local_latents = enc_weight.shape[2]
     blocks = local_latents // BLOCK
     pair_slots = (blocks + 1) // 2
+    kept = min(KEPT_PAIRS, pair_slots)
+    more = max(pair_slots - kept, 1)
     layers, latents = lax.axis_size("layer"), lax.axis_size("latent")
     layer, latent = lax.axis_index("layer"), lax.axis_index("latent")
     core = latent % 2
@@ -144,28 +197,33 @@
     near_target = swap(target, "layer", 1)
     chip_bits = [1 << s for s in range((chips - 1).bit_length(), 0, -1)]
 
+    dec_hbm = pltpu.with_memory_space_constraint(dec_weight[0], pltpu.HBM)
     vmem = pl.BlockSpec(memory_space=pltpu.VMEM)
     smem = pl.BlockSpec(memory_space=pltpu.SMEM)
     anyw = pl.BlockSpec(memory_space=pl.ANY)
     keep, send, dec_kept, ids = pl.pallas_call(
         encode_decode,
         out_shape=(
-            jax.ShapeDtypeStruct((rows, model_width), F32),
-            jax.ShapeDtypeStruct((rows, model_width), BF16),
-            pltpu.VMEM((pair_slots, PAIR, model_width), BF16),
-            jax.ShapeDtypeStruct((1, blocks + 1), jnp.int32),
+            pltpu.VMEM((rows, model_width), F32),
+            pltpu.VMEM((rows, model_width), BF16),
+            pltpu.VMEM((kept, PAIR, model_width), BF16),
+            pltpu.SMEM((1, blocks + 1), jnp.int32),
         ),
-        in_specs=[smem, smem, vmem, vmem, anyw, anyw],
+        in_specs=[smem, smem, anyw, anyw, anyw, anyw],
         out_specs=(vmem, vmem, vmem, smem),
         scratch_shapes=[
+            pltpu.VMEM((tok_rows, model_width), BF16),
+            pltpu.VMEM((1, local_latents), F32),
+            pltpu.VMEM((more, PAIR, model_width), BF16),
             pltpu.VMEM((pair_slots, model_width, PAIR), BF16),
             pltpu.VMEM((tok_rows, model_width), F32),
+            pltpu.SemaphoreType.DMA((2,)),
             pltpu.SemaphoreType.DMA((blocks,)),
             pltpu.SemaphoreType.DMA((blocks,)),
         ],
-        compiler_params=pltpu.CompilerParams(vmem_limit_bytes=48 << 20),
+        compiler_params=pltpu.CompilerParams(vmem_limit_bytes=32 << 20),
         name="encode_decode",
-    )(block_list, block_count, residuals[0], enc_bias, enc_weight[0], dec_weight[0])
+    )(block_list, block_count, *[pltpu.with_memory_space_constraint(a, pltpu.HBM) for a in (residuals[0], enc_bias, enc_weight[0])], dec_hbm)
 
     held = keep + swap(send, "latent", 1).astype(F32)
     for bit in chip_bits[:-1]:
@@ -216,33 +274,46 @@
         all_square = all_square + there_square
 
     grad_in = after.astype(BF16)
+    before, grad_in = lax.optimization_barrier((before, grad_in))
     fitted = gain * before
     error_term = fitted - target.astype(F32)
-    loss = jnp.sum(error_term * error_term).reshape(1, 1)
-
+    loss = jnp.sum(error_term * error_term, axis=0, keepdims=True)
+    recon = fitted.astype(BF16)
+
+    other_loss = swap(loss, "latent", 1)
+    loss = loss + other_loss
+    chip_loss = jnp.zeros_like(loss)
     for bit in reversed(chip_bits):
         upper = (latent & bit) != 0
         got = swap(grad_in, "latent", bit)
+        if bit != chip_bits[0]:
+            loss = loss + swap(loss, "latent", bit)
+        else:
+            chip_loss = swap(loss, "latent", bit)
         grad_in = jnp.concatenate([jnp.where(upper, got, grad_in), jnp.where(upper, grad_in, got)], axis=1)
-        loss = loss + swap(loss, "latent", bit)
     other_rows = swap(grad_in, "latent", 1)
-    loss = (loss + swap(loss, "latent", 1)) / (tok_rows * model_width)
-
-    recon = fitted.astype(BF16)
+
     columns = width // 2
     stay = part(recon, core * columns, columns, 1)
     got = swap(part(recon, (1 - core) * columns, columns, 1), "latent", 1)
     recon = jnp.concatenate([jnp.where(core == 0, stay, got), jnp.where(core == 0, got, stay)], axis=0)
 
-    code_grad = pl.pallas_call(
+    code_grad, loss = pl.pallas_call(
         code_gradient,
-        out_shape=jax.ShapeDtypeStruct((tok_rows, local_latents), BF16),
-        in_specs=[smem, vmem, vmem, vmem],
-        out_specs=vmem,
-        scratch_shapes=[pltpu.VMEM((tok_rows, model_width), BF16)],
-        compiler_params=pltpu.CompilerParams(vmem_limit_bytes=24 << 20),
+        out_shape=(
+            jax.ShapeDtypeStruct((tok_rows, local_latents), BF16),
+            jax.ShapeDtypeStruct((1, 1), F32),
+        ),
+        in_specs=[smem, vmem, vmem, vmem, vmem, vmem, anyw],
+        out_specs=(vmem, vmem),
+        scratch_shapes=[
+            pltpu.VMEM((tok_rows, model_width), BF16),
+            pltpu.VMEM((more, PAIR, model_width), BF16),
+            pltpu.SemaphoreType.DMA((blocks,)),
+        ],
+        compiler_params=pltpu.CompilerParams(vmem_limit_bytes=16 << 20),
         name="code_gradient",
-    )(ids, grad_in, other_rows, pltpu.with_memory_space_constraint(dec_kept, pltpu.VMEM))
+    )(ids, grad_in, other_rows, loss, chip_loss, pltpu.with_memory_space_constraint(dec_kept, pltpu.VMEM), dec_hbm)
     return recon[None], code_grad[None], loss
 
 

time: 57.7 us -> 44.5 us (0.77)
  the two profiles are of different devices: /device:TPU:1 before, /device:TPU:0 now
where the time goes in v2:
time: 44.5 us; the launch traced here: 44 us
  waiting for transfers between devices  17.5 us (39%)
  starting transfers between devices  15 us (34%)
  Pallas kernels  7.23 us (16%)
  local copies, waits for them, and re-layouts  1.67 us (4%)
  between operations  1.43 us (3%)
  other arithmetic  1.15 us (3%)
    ppermute x12, starting transfers between devices, swap(): return lax.ppermute(value, axis, [(i, i ^ bit) for i in range(size)])  12.2 us
    ppermute x12, waiting for transfers between devices, swap(): return lax.ppermute(value, axis, [(i, i ^ bit) for i in range(size)])  12 us
    ppermute x1, waiting for transfers between devices, swap_both(): return lax.ppermute(value, ('layer', 'latent'), pairs)  5.55 us
    pallas_call x1, Pallas kernels, local(): pl.pallas_call(encode_decode, out_shape=(pltpu.VMEM((rows, model_width),...  4.51 us
    ppermute x1, starting transfers between devices, swap_both(): return lax.ppermute(value, ('layer', 'latent'), pairs)  2.77 us
    pallas_call x1, Pallas kernels, local(): pl.pallas_call(code_gradient, out_shape=(jax.ShapeDtypeStruct((tok_rows,...  2.73 us
    unnamed x7, local copies, waits for them, and re-layouts  1.45 us
  transfers between devices with their start and end apart: 13, of which 7 were waited for; matrix products, arithmetic and copies ran while one was open for 3% of the time, Pallas kernels for 0%

profile of v2, /device:TPU:0, one launch (start us, length us, event | category | flops | bytes accessed | tf_op | source)
XLA Modules:
  0.0 44.0 jit_solution(4767874101321799148)
XLA Ops:
  1.3 0.6 %copy-done = s32[1,1,24]{2,1,0:T(1,128)S(1)} copy-done((s32[1,1,24]{2,1,0:T(1,128)S(1)}, s32[1,1,24]{2,1,0:T(1,128)}, u32[]{:S(2)}) %copy-start) | copy-done | bytes 120
  1.9 4.5 %encode_decode.1 = (f32[64,2304]{1,0:T(8,128)S(1)}, bf16[64,2304]{1,0:T(8,128)(2,1)S(1)}, bf16[1,256,2304]{2,1,0:T(8,128)(2,1)S(1)}, s32[1,17]{1,0:T(1,128)S(4)}) custom-call(s32[1,1,24]{2,1,0:T(1,128)S(1)} %copy-done, s32[1,1]{1,0:T(1,128)S(6)} %copy.12.count_ref, bf16[128,2304]{1,0:T(8,128)(2,1)} %bitcast.17, f32[1,2048]{1,0:T(1,128)} %bias_any.1, ...), custom_call_target="tpu_custom_call" | custom-call | tf_op jit(solution)/shard_map/encode_decode/pallas_call | solution.py:204
  6.5 2.2 %collective-permute-start = (bf16[64,2304]{1,0:T(8,128)(2,1)S(1)}, bf16[64,2304]{1,0:T(8,128)(2,1)S(1)}, u32[]{:S(2)}, u32[]{:S(2)}) collective-permute-start(bf16[64,2304]{1,0:T(8,128)(2,1)S(1)} %get-tuple-element.12), channel_id=1, source_target_pairs={{0,1},{1,0},{2,3},{3,2},{4,5},{5,4},{6,7},{7,6},{8,9},{9,8},{10,11... | collective-permute-start | bytes 884744 | tf_op jit(solution)/shard_map/ppermute | solution.py:162
  8.8 1.8 %collective-permute-start.5 = (bf16[64,1152]{1,0:T(8,128)(2,1)S(1)}, bf16[64,1152]{1,0:T(8,128)(2,1)S(1)}, u32[]{:S(2)}, u32[]{:S(2)}) collective-permute-start(bf16[64,1152]{1,0:T(8,128)(2,1)S(1)} %dynamic-slice_bitcast_fusion), channel_id=1, source_target_pairs={{0,4},{4,0},{8,12},{12,8},{1,5},{5,1},{9,13},{13,9},{2,6},{6,2},{1... | collective-permute-start | bytes 442376 | tf_op jit(solution)/shard_map/ppermute | solution.py:162
  10.6 0.3 collective-permute-start.4
  11.0 2.8 %collective-permute-start.3 = (bf16[64,1152]{1,0:T(8,128)(2,1)S(1)}, bf16[64,1152]{1,0:T(8,128)(2,1)S(1)}, u32[]{:S(2)}, u32[]{:S(2)}) collective-permute-start(bf16[64,1152]{1,0:T(8,128)(2,1)S(1)} %select_convert_fusion.1), channel_id=1, source_target_pairs={{0,6},{1,7},{2,4},{3,5},{4,2},{5,3},{6,0},{7,1},{8,14},{9,15},{10,... | collective-permute-start | bytes 442376 | tf_op jit(solution)/shard_map/ppermute | solution.py:170
  13.8 0.5 %collective-permute-start.1 = (bf16[64,1152]{1,0:T(8,128)(2,1)S(1)}, bf16[64,1152]{1,0:T(8,128)(2,1)S(1)}, u32[]{:S(2)}, u32[]{:S(2)}) collective-permute-start(bf16[64,1152]{1,0:T(8,128)(2,1)S(1)} %select_convert_fusion.1), channel_id=1, source_target_pairs={{0,2},{1,3},{2,0},{3,1},{4,6},{5,7},{6,4},{7,5},{8,10},{9,11},{10,... | collective-permute-start | bytes 442376 | tf_op jit(solution)/shard_map/ppermute | solution.py:162
  14.3 0.8 %collective-permute-start.2 = (bf16[64,1152]{1,0:T(8,128)(2,1)S(1)}, bf16[64,1152]{1,0:T(8,128)(2,1)S(1)}, u32[]{:S(2)}, u32[]{:S(2)}) collective-permute-start(bf16[64,1152]{1,0:T(8,128)(2,1)S(1)} %get-tuple-element.27), channel_id=1, source_target_pairs={{0,4},{4,0},{8,12},{12,8},{1,5},{5,1},{9,13},{13,9},{2,6},{6,2},{1... | collective-permute-start | bytes 442376 | tf_op jit(solution)/shard_map/ppermute | solution.py:162
  15.3 5.6 %collective-permute-done.3 = bf16[64,1152]{1,0:T(8,128)(2,1)S(1)} collective-permute-done((bf16[64,1152]{1,0:T(8,128)(2,1)S(1)}, bf16[64,1152]{1,0:T(8,128)(2,1)S(1)}, u32[]{:S(2)}, u32[]{:S(2)}) %collective-permute-start.3) | collective-permute-done | bytes 147488 | tf_op jit(solution)/shard_map/ppermute | solution.py:170
  20.8 1.1 %collective-permute-done.2 = bf16[64,1152]{1,0:T(8,128)(2,1)S(1)} collective-permute-done((bf16[64,1152]{1,0:T(8,128)(2,1)S(1)}, bf16[64,1152]{1,0:T(8,128)(2,1)S(1)}, u32[]{:S(2)}, u32[]{:S(2)}) %collective-permute-start.2) | collective-permute-done | bytes 147488 | tf_op jit(solution)/shard_map/ppermute | solution.py:162
  22.0 0.4 collective-permute-done.1
  22.3 0.3 select_convert_fusion
  22.6 1.9 %collective-permute-start.6 = (bf16[64,1152]{1,0:T(8,128)(2,1)S(1)}, bf16[64,1152]{1,0:T(8,128)(2,1)S(1)}, u32[]{:S(2)}, u32[]{:S(2)}) collective-permute-start(bf16[64,1152]{1,0:T(8,128)(2,1)S(1)} %select_convert_fusion), channel_id=1, source_target_pairs={{0,8},{4,12},{8,0},{12,4},{1,9},{5,13},{9,1},{13,5},{2,10},{6,14},... | collective-permute-start | bytes 442376 | tf_op jit(solution)/shard_map/ppermute | solution.py:162
  24.4 1.1 %collective-permute-start.7 = (f32[1,1152]{1,0:T(1,128)S(1)}, f32[1,1152]{1,0:T(1,128)S(1)}, u32[]{:S(2)}, u32[]{:S(2)}) collective-permute-start(f32[1,1152]{1,0:T(1,128)S(1)} %get-tuple-element.37), channel_id=1, source_target_pairs={{0,8},{4,12},{8,0},{12,4},{1,9},{5,13},{9,1},{13,5},{2,10},{6,14},... | collective-permute-start | bytes 13832 | tf_op jit(solution)/shard_map/ppermute | solution.py:162
  25.6 6.1 %collective-permute-done.7 = f32[1,1152]{1,0:T(1,128)S(1)} collective-permute-done((f32[1,1152]{1,0:T(1,128)S(1)}, f32[1,1152]{1,0:T(1,128)S(1)}, u32[]{:S(2)}, u32[]{:S(2)}) %collective-permute-start.7) | collective-permute-done | bytes 4640 | tf_op jit(solution)/shard_map/ppermute | solution.py:162
  31.7 0.4 fusion.4
  32.1 0.1 fusion.2
  32.4 0.6 %collective-permute-start.8 = (bf16[64,576]{1,0:T(8,128)(2,1)S(1)}, bf16[64,576]{1,0:T(8,128)(2,1)S(1)}, u32[]{:S(2)}, u32[]{:S(2)}) collective-permute-start(bf16[64,576]{1,0:T(8,128)(2,1)S(1)} %constant_dynamic-slice_fusion), channel_id=1, source_target_pairs={{0,1},{1,0},{2,3},{3,2},{4,5},{5,4},{6,7},{7,6},{8,9},{9,8},{10,11... | collective-permute-start | bytes 221192 | tf_op jit(solution)/shard_map/ppermute | solution.py:162
  33.0 2.4 %collective-permute-start.9 = (bf16[64,1152]{1,0:T(8,128)(2,1)S(1)}, bf16[64,1152]{1,0:T(8,128)(2,1)S(1)}, u32[]{:S(2)}, u32[]{:S(2)}) collective-permute-start(bf16[64,1152]{1,0:T(8,128)(2,1)S(1)} %get-tuple-element.15), channel_id=1, source_target_pairs={{0,2},{1,3},{2,0},{3,1},{4,6},{5,7},{6,4},{7,5},{8,10},{9,11},{10,... | collective-permute-start | bytes 442376 | tf_op jit(solution)/shard_map/ppermute | solution.py:162
  35.4 0.5 %collective-permute-start.12 = (f32[1,1152]{1,0:T(1,128)S(1)}, f32[1,1152]{1,0:T(1,128)S(1)}, u32[]{:S(2)}, u32[]{:S(2)}) collective-permute-start(f32[1,1152]{1,0:T(1,128)S(1)} %reshape_add_fusion.loss_ref), channel_id=1, source_target_pairs={{0,2},{1,3},{2,0},{3,1},{4,6},{5,7},{6,4},{7,5},{8,10},{9,11},{10,... | collective-permute-start | bytes 13832 | tf_op jit(solution)/shard_map/ppermute | solution.py:162
  35.9 3.6 %collective-permute-done.9 = bf16[64,1152]{1,0:T(8,128)(2,1)S(1)} collective-permute-done((bf16[64,1152]{1,0:T(8,128)(2,1)S(1)}, bf16[64,1152]{1,0:T(8,128)(2,1)S(1)}, u32[]{:S(2)}, u32[]{:S(2)}) %collective-permute-start.9) | collective-permute-done | bytes 147488 | tf_op jit(solution)/shard_map/ppermute | solution.py:162
  39.8 0.8 %copy.11 = bf16[1,128,576]{1,2,0:T(8,128)(2,1)} copy(bf16[1,128,576]{2,1,0:T(8,128)(2,1)S(1)} %maximum_bitcast_fusion) | data formatting | bytes 294912
  40.6 0.6 %collective-permute-done.10.other_ref = bf16[64,2304]{1,0:T(8,128)(2,1)S(1)} collective-permute-done((bf16[64,2304]{1,0:T(8,128)(2,1)S(1)}, bf16[64,2304]{1,0:T(8,128)(2,1)S(1)}, u32[]{:S(2)}, u32[]{:S(2)}) %collective-permute-start.10) | collective-permute-done | bytes 294944 | tf_op jit(solution)/shard_map/ppermute | solution.py:162
  41.2 2.7 %code_gradient.1 = (bf16[128,2048]{1,0:T(8,128)(2,1)}, f32[1,1]{1,0:T(1,128)}) custom-call(s32[1,17]{1,0:T(1,128)S(4)} %get-tuple-element.14.ids_ref, bf16[64,2304]{1,0:T(8,128)(2,1)S(1)} %pad_maximum_fusion.own_ref, bf16[64,2304]{1,0:T(8,128)(2,1)S(1)} %collective-permute-done.10.other_ref, f32[1,1152]{1,0:T(1,128)S(1)} %reshape_add_fusion.loss_ref, ...), custom_call_target="tpu_custom_call" | custom-call | tf_op jit(solution)/shard_map/code_gradient/pallas_call | solution.py:301
  (28 shorter events, 0.8 us)
Async XLA Ops:
  1.3 0.7 %copy-start = (s32[1,1,24]{2,1,0:T(1,128)S(1)}, s32[1,1,24]{2,1,0:T(1,128)}, u32[]{:S(2)}) copy-start(s32[1,1,24]{2,1,0:T(1,128)} %list_ref.1) | copy-start | bytes 292
  1.9 6.7 %copy-start.1 = (bf16[1,128,2304]{2,1,0:T(8,128)(2,1)S(1)}, bf16[1,128,2304]{2,1,0:T(8,128)(2,1)}, u32[]{:S(2)}) copy-start(bf16[1,128,2304]{2,1,0:T(8,128)(2,1)} %param.9) | copy-start | bytes 1769476
  1.9 8.7 %copy-start.2 = (f32[1,2304]{1,0:T(1,128)S(1)}, f32[1,2304]{1,0:T(1,128)}, u32[]{:S(2)}) copy-start(f32[1,2304]{1,0:T(1,128)} %param.13) | copy-start | bytes 27652
  6.5 4.4 %collective-permute-start = (bf16[64,2304]{1,0:T(8,128)(2,1)S(1)}, bf16[64,2304]{1,0:T(8,128)(2,1)S(1)}, u32[]{:S(2)}, u32[]{:S(2)}) collective-permute-start(bf16[64,2304]{1,0:T(8,128)(2,1)S(1)} %get-tuple-element.12), channel_id=1, source_target_pairs={{0,1},{1,0},{2,3},{3,2},{4,5},{5,4},{6,7},{7,6},{8,9},{9,8},{10,11... | collective-permute-start | bytes 884744 | tf_op jit(solution)/shard_map/ppermute | solution.py:162
  8.8 6.5 %collective-permute-start.5 = (bf16[64,1152]{1,0:T(8,128)(2,1)S(1)}, bf16[64,1152]{1,0:T(8,128)(2,1)S(1)}, u32[]{:S(2)}, u32[]{:S(2)}) collective-permute-start(bf16[64,1152]{1,0:T(8,128)(2,1)S(1)} %dynamic-slice_bitcast_fusion), channel_id=1, source_target_pairs={{0,4},{4,0},{8,12},{12,8},{1,5},{5,1},{9,13},{13,9},{2,6},{6,2},{1... | collective-permute-start | bytes 442376 | tf_op jit(solution)/shard_map/ppermute | solution.py:162
  10.6 4.6 %collective-permute-start.4 = (f32[1,1152]{1,0:T(1,128)S(1)}, f32[1,1152]{1,0:T(1,128)S(1)}, u32[]{:S(2)}, u32[]{:S(2)}) collective-permute-start(f32[1,1152]{1,0:T(1,128)S(1)} %constant_dynamic-slice_fusion.1), channel_id=1, source_target_pairs={{0,4},{4,0},{8,12},{12,8},{1,5},{5,1},{9,13},{13,9},{2,6},{6,2},{1... | collective-permute-start | bytes 13832 | tf_op jit(solution)/shard_map/ppermute | solution.py:162
  11.0 9.8 %collective-permute-start.3 = (bf16[64,1152]{1,0:T(8,128)(2,1)S(1)}, bf16[64,1152]{1,0:T(8,128)(2,1)S(1)}, u32[]{:S(2)}, u32[]{:S(2)}) collective-permute-start(bf16[64,1152]{1,0:T(8,128)(2,1)S(1)} %select_convert_fusion.1), channel_id=1, source_target_pairs={{0,6},{1,7},{2,4},{3,5},{4,2},{5,3},{6,0},{7,1},{8,14},{9,15},{10,... | collective-permute-start | bytes 442376 | tf_op jit(solution)/shard_map/ppermute | solution.py:170
  13.8 8.5 %collective-permute-start.1 = (bf16[64,1152]{1,0:T(8,128)(2,1)S(1)}, bf16[64,1152]{1,0:T(8,128)(2,1)S(1)}, u32[]{:S(2)}, u32[]{:S(2)}) collective-permute-start(bf16[64,1152]{1,0:T(8,128)(2,1)S(1)} %select_convert_fusion.1), channel_id=1, source_target_pairs={{0,2},{1,3},{2,0},{3,1},{4,6},{5,7},{6,4},{7,5},{8,10},{9,11},{10,... | collective-permute-start | bytes 442376 | tf_op jit(solution)/shard_map/ppermute | solution.py:162
  14.3 7.6 %collective-permute-start.2 = (bf16[64,1152]{1,0:T(8,128)(2,1)S(1)}, bf16[64,1152]{1,0:T(8,128)(2,1)S(1)}, u32[]{:S(2)}, u32[]{:S(2)}) collective-permute-start(bf16[64,1152]{1,0:T(8,128)(2,1)S(1)} %get-tuple-element.27), channel_id=1, source_target_pairs={{0,4},{4,0},{8,12},{12,8},{1,5},{5,1},{9,13},{13,9},{2,6},{6,2},{1... | collective-permute-start | bytes 442376 | tf_op jit(solution)/shard_map/ppermute | solution.py:162
  22.6 9.1 %collective-permute-start.6 = (bf16[64,1152]{1,0:T(8,128)(2,1)S(1)}, bf16[64,1152]{1,0:T(8,128)(2,1)S(1)}, u32[]{:S(2)}, u32[]{:S(2)}) collective-permute-start(bf16[64,1152]{1,0:T(8,128)(2,1)S(1)} %select_convert_fusion), channel_id=1, source_target_pairs={{0,8},{4,12},{8,0},{12,4},{1,9},{5,13},{9,1},{13,5},{2,10},{6,14},... | collective-permute-start | bytes 442376 | tf_op jit(solution)/shard_map/ppermute | solution.py:162
  24.4 7.2 %collective-permute-start.7 = (f32[1,1152]{1,0:T(1,128)S(1)}, f32[1,1152]{1,0:T(1,128)S(1)}, u32[]{:S(2)}, u32[]{:S(2)}) collective-permute-start(f32[1,1152]{1,0:T(1,128)S(1)} %get-tuple-element.37), channel_id=1, source_target_pairs={{0,8},{4,12},{8,0},{12,4},{1,9},{5,13},{9,1},{13,5},{2,10},{6,14},... | collective-permute-start | bytes 13832 | tf_op jit(solution)/shard_map/ppermute | solution.py:162
  32.3 3.1 %collective-permute-start.11 = (f32[1,1152]{1,0:T(1,128)S(1)}, f32[1,1152]{1,0:T(1,128)S(1)}, u32[]{:S(2)}, u32[]{:S(2)}) collective-permute-start(f32[1,1152]{1,0:T(1,128)S(1)} %broadcast_in_dim.10), channel_id=1, source_target_pairs={{0,1},{1,0},{2,3},{3,2},{4,5},{5,4},{6,7},{7,6},{8,9},{9,8},{10,11... | collective-permute-start | bytes 13832 | tf_op jit(solution)/shard_map/ppermute | solution.py:162
  32.4 7.2 %collective-permute-start.8 = (bf16[64,576]{1,0:T(8,128)(2,1)S(1)}, bf16[64,576]{1,0:T(8,128)(2,1)S(1)}, u32[]{:S(2)}, u32[]{:S(2)}) collective-permute-start(bf16[64,576]{1,0:T(8,128)(2,1)S(1)} %constant_dynamic-slice_fusion), channel_id=1, source_target_pairs={{0,1},{1,0},{2,3},{3,2},{4,5},{5,4},{6,7},{7,6},{8,9},{9,8},{10,11... | collective-permute-start | bytes 221192 | tf_op jit(solution)/shard_map/ppermute | solution.py:162
  33.0 6.5 %collective-permute-start.9 = (bf16[64,1152]{1,0:T(8,128)(2,1)S(1)}, bf16[64,1152]{1,0:T(8,128)(2,1)S(1)}, u32[]{:S(2)}, u32[]{:S(2)}) collective-permute-start(bf16[64,1152]{1,0:T(8,128)(2,1)S(1)} %get-tuple-element.15), channel_id=1, source_target_pairs={{0,2},{1,3},{2,0},{3,1},{4,6},{5,7},{6,4},{7,5},{8,10},{9,11},{10,... | collective-permute-start | bytes 442376 | tf_op jit(solution)/shard_map/ppermute | solution.py:162
  35.4 5.2 %collective-permute-start.12 = (f32[1,1152]{1,0:T(1,128)S(1)}, f32[1,1152]{1,0:T(1,128)S(1)}, u32[]{:S(2)}, u32[]{:S(2)}) collective-permute-start(f32[1,1152]{1,0:T(1,128)S(1)} %reshape_add_fusion.loss_ref), channel_id=1, source_target_pairs={{0,2},{1,3},{2,0},{3,1},{4,6},{5,7},{6,4},{7,5},{8,10},{9,11},{10,... | collective-permute-start | bytes 13832 | tf_op jit(solution)/shard_map/ppermute | solution.py:162
  39.6 1.6 %collective-permute-start.10 = (bf16[64,2304]{1,0:T(8,128)(2,1)S(1)}, bf16[64,2304]{1,0:T(8,128)(2,1)S(1)}, u32[]{:S(2)}, u32[]{:S(2)}) collective-permute-start(bf16[64,2304]{1,0:T(8,128)(2,1)S(1)} %pad_maximum_fusion.own_ref), channel_id=1, source_target_pairs={{0,1},{1,0},{2,3},{3,2},{4,5},{5,4},{6,7},{7,6},{8,9},{9,8},{10,11... | collective-permute-start | bytes 884744 | tf_op jit(solution)/shard_map/ppermute | solution.py:162

commit v3 on v1

v3 whole, which is shorter than its diff:
```python
import functools

import jax
import jax.numpy as jnp
from jax import lax
from jax.experimental import pallas as pl
from jax.experimental.pallas import tpu as pltpu
from jax.sharding import PartitionSpec as P

BLOCK = 128
PAIR = 2 * BLOCK
KEPT_PAIRS = 3
F32 = jnp.float32
BF16 = jnp.bfloat16


def encode_decode(
    list_any, count_ref, x_any, bias_any, enc_ref, dec_ref, keep_ref, send_ref, ids_ref,
    list_ref, x_ref, bias_ref, enc_held, dec_held, codes, total, in_sem, enc_sem, dec_sem,
):
    blocks = enc_ref.shape[1] // BLOCK
    list_load = pltpu.make_async_copy(list_any, list_ref, in_sem.at[0])
    list_load.start()
    loads = [pltpu.make_async_copy(x_any, x_ref, in_sem.at[1]), pltpu.make_async_copy(bias_any, bias_ref, in_sem.at[2])]
    for load in loads:
        load.start()
    where = lax.axis_index("latent")
    first = where * blocks
    slots = list_ref.shape[2]
    count = count_ref[0, 0]
    total[...] = jnp.zeros_like(total)

    def copies(block, n):
        pair, half = lax.div(n, 2), pl.multiple_of(lax.rem(n, 2) * BLOCK, BLOCK)
        source = pl.ds(pl.multiple_of(block * BLOCK, BLOCK), BLOCK)
        return (
            pltpu.make_async_copy(enc_ref.at[:, source], enc_held.at[pair, :, pl.ds(half, BLOCK)], enc_sem.at[n]),
            pltpu.make_async_copy(dec_ref.at[source, :], dec_held.at[pair, pl.ds(half, BLOCK), :], dec_sem.at[n]),
        )

    def look(slot, n):
        block = list_ref[0, 0, slot] - first
        live = (slot < count) & (block >= 0) & (block < blocks)

        @pl.when(live)
        def _():
            ids_ref[0, n] = block
            for copy in copies(block, n):
                copy.start()

        return n + live.astype(jnp.int32)

    list_load.wait()
    live_count = lax.fori_loop(0, slots, look, jnp.int32(0))
    ids_ref[0, blocks] = live_count
    pairs = lax.div(live_count + 1, 2)

    @pl.when(lax.rem(live_count, 2) == 1)
    def _():
        dec_held[pairs - 1, pl.ds(BLOCK, BLOCK), :] = jnp.zeros((BLOCK, dec_held.shape[2]), BF16)
        ids_ref[0, live_count] = ids_ref[0, live_count - 1]

    for load in loads:
        load.wait()

    def arrive(pair, which):
        n = 2 * pair
        copies(ids_ref[0, n], n)[which].wait()

        @pl.when(n + 1 < live_count)
        def _():
            copies(ids_ref[0, n + 1], n + 1)[which].wait()

    def encode(pair):
        n = 2 * pair
        bias = jnp.concatenate(
            [bias_ref[:, pl.ds(pl.multiple_of(ids_ref[0, i] * BLOCK, BLOCK), BLOCK)] for i in (n, n + 1)], axis=1
        )
        pre_act = jnp.dot(x_ref[...], enc_held[pair], preferred_element_type=F32) + bias
        lane = lax.broadcasted_iota(jnp.int32, pre_act.shape, 1)
        used = (lane < BLOCK) | (n + 1 < live_count)
        codes[lax.rem(pair, 2)] = jnp.where(used, jnp.maximum(pre_act, 0.0), 0.0).astype(BF16)

    def decode(pair):
        total[...] += jnp.dot(codes[lax.rem(pair, 2)], dec_held[pair], preferred_element_type=F32)

    def step(pair, carry):
        arrive(pair, 0)
        arrive(pair - 1, 1)
        encode(pair)
        decode(pair - 1)
        return carry

    @pl.when(pairs > 0)
    def _():
        arrive(0, 0)
        encode(0)
        lax.fori_loop(1, pairs, step, 0)
        arrive(pairs - 1, 1)
        decode(pairs - 1)

    rows = keep_ref.shape[0]
    core = lax.rem(where, 2)
    keep_ref[...] = total[pl.ds(pl.multiple_of(core * rows, rows), rows), :]
    send_ref[...] = total[pl.ds(pl.multiple_of((1 - core) * rows, rows), rows), :].astype(BF16)


def finish(
    got_ref, before_ref, after_ref, all_ref, there_square_ref, after_square_ref, gain_ref, target_ref,
    message_ref, stay_ref, send_ref,
):
    got = got_ref[...].astype(F32)
    width = got.shape[1]
    low = (lax.axis_index("layer") & (lax.axis_size("layer") // 2)) == 0
    fitted = gain_ref[...] * jnp.where(low, before_ref[...], before_ref[...] + got)
    error_term = fitted - target_ref[...].astype(F32)
    squares = error_term * error_term
    added = functools.reduce(add_terms, [squares[:, i : i + BLOCK] for i in range(0, width - BLOCK + 1, BLOCK)])
    rest = width % BLOCK
    if rest:
        zeros = jnp.zeros((squares.shape[0], BLOCK - rest), F32)
        added = added + jnp.concatenate([squares[:, width - rest :], zeros], axis=1)
    entering = jnp.where(low, there_square_ref[...] * all_ref[...] + got, after_square_ref[...] * got)
    message_ref[:, :width] = (after_ref[...] + entering).astype(BF16)
    message_ref[:, width:] = added.astype(BF16)
    left, right = fitted[:, : width // 2].astype(BF16), fitted[:, width // 2 :].astype(BF16)
    first = (lax.axis_index("latent") & 1) == 0
    stay_ref[...] = jnp.where(first, left, right)
    send_ref[...] = jnp.where(first, right, left)


def add_terms(one, two):
    return one + two


def rows_of(dec_ref, block, half):
    cut = dec_ref.shape[1] // 2
    return dec_ref.at[pl.ds(pl.multiple_of(block * BLOCK, BLOCK), BLOCK), pl.ds(pl.multiple_of(half * cut, cut), cut)]


def place_of(n):
    return lax.div(n, 2), pl.ds(pl.multiple_of(lax.rem(n, 2) * BLOCK, BLOCK), BLOCK)


def by_core(core, mine, theirs, held):
    rows = mine.shape[0]
    held[pl.ds(pl.multiple_of(core * rows, rows), rows), :] = mine
    held[pl.ds(pl.multiple_of((1 - core) * rows, rows), rows), :] = theirs


def times_rows(grad, rows):
    return lax.dot_general(grad, rows, (((1,), (1,)), ((), ())), preferred_element_type=F32)


def near_gradient(top, ids_ref, own_ref, near_ref, dec_ref, part_ref, far_kept, grad, dec_near, near_sem, far_sem):
    blocks = near_sem.shape[0]
    kept, _, cut = far_kept.shape
    latent = lax.axis_index("latent")
    here = lax.div(latent & top, top)
    live_count = ids_ref[0, blocks]
    far_count = jnp.minimum(live_count, 2 * kept)

    def near_copy(n):
        pair, place = place_of(n)
        return pltpu.make_async_copy(rows_of(dec_ref, ids_ref[0, n], here), dec_near.at[pair, place, :], near_sem.at[n])

    def far_copy(n):
        pair, place = place_of(n)
        return pltpu.make_async_copy(rows_of(dec_ref, ids_ref[0, n], 1 - here), far_kept.at[pair, place, :], far_sem.at[n])

    lax.fori_loop(0, live_count, lambda n, c: (near_copy(n).start(), c)[1], 0)
    lax.fori_loop(0, far_count, lambda n, c: (far_copy(n).start(), c)[1], 0)
    by_core(latent & 1, own_ref[:, :cut], near_ref[:, :cut], grad)

    def step(pair, carry):
        n = 2 * pair
        near_copy(n).wait()
        pl.when(n + 1 < live_count)(lambda: near_copy(n + 1).wait())
        part_ref[pair] = times_rows(grad[...], dec_near[pair])
        return carry

    lax.fori_loop(0, lax.div(live_count + 1, 2), step, 0)
    lax.fori_loop(0, far_count, lambda n, c: (far_copy(n).wait(), c)[1], 0)


def code_gradient(
    top, ids_ref, own_ref, near_ref, got_ref, far_ref, stay_ref, part_ref, far_kept, dec_ref,
    out_ref, recon_ref, mean_ref, grad, fitted, dec_far, far_sem,
):
    blocks = far_sem.shape[0]
    kept, _, cut = far_kept.shape
    latent = lax.axis_index("latent")
    there = 1 - lax.div(latent & top, top)
    core = latent & 1
    live_count = ids_ref[0, blocks]
    pairs = lax.div(live_count + 1, 2)

    def far_copy(n):
        pair, place = place_of(n - 2 * kept)
        return pltpu.make_async_copy(rows_of(dec_ref, ids_ref[0, n], there), dec_far.at[pair, place, :], far_sem.at[n])

    lax.fori_loop(2 * kept, live_count, lambda n, c: (far_copy(n).start(), c)[1], 0)
    by_core(core, got_ref[:, :cut], far_ref[:, :cut], grad)
    out_ref[...] = jnp.zeros_like(out_ref)

    def store(pair, product):
        n = 2 * pair
        out_ref[:, pl.ds(pl.multiple_of(ids_ref[0, n] * BLOCK, BLOCK), BLOCK)] = product[:, :BLOCK]

        @pl.when(n + 1 < live_count)
        def _():
            out_ref[:, pl.ds(pl.multiple_of(ids_ref[0, n + 1] * BLOCK, BLOCK), BLOCK)] = product[:, BLOCK:]

    def step(pair, carry):
        store(pair, (part_ref[pair] + times_rows(grad[...], far_kept[pair])).astype(BF16))
        return carry

    def fetched(pair, carry):
        n = 2 * pair
        far_copy(n).wait()
        pl.when(n + 1 < live_count)(lambda: far_copy(n + 1).wait())
        store(pair, (part_ref[pair] + times_rows(grad[...], dec_far[pair - kept])).astype(BF16))
        return carry

    lax.fori_loop(0, jnp.minimum(pairs, kept), step, 0)
    lax.fori_loop(kept, pairs, fetched, 0)
    columns = stay_ref.shape[1]
    by_core(core, stay_ref[...].astype(F32), near_ref[:, cut + BLOCK :].astype(F32), fitted)
    recon_ref[...] = jnp.transpose(fitted[...]).astype(BF16)
    squares = sum(ref[:, cut : cut + BLOCK].astype(F32) for ref in (own_ref, near_ref, got_ref, far_ref))
    total = jnp.sum(jnp.sum(squares, axis=0, keepdims=True), axis=1, keepdims=True)
    mean_ref[...] = total / (grad.shape[0] * 2 * cut)


def swap(value, axis, bit):
    size = lax.axis_size(axis)
    return lax.ppermute(value, axis, [(i, i ^ bit) for i in range(size)])


def in_hbm(value):
    return pltpu.with_memory_space_constraint(value, pltpu.HBM)


def part(value, start, size, axis):
    return lax.dynamic_slice_in_dim(value, start, size, axis)


def local(residuals, targets, enc_weight, enc_bias, dec_weight, out_gain, block_list, block_count):
    tok_rows, model_width = residuals.shape[1:]
    local_latents = enc_weight.shape[2]
    blocks = local_latents // BLOCK
    pair_slots = (blocks + 1) // 2
    kept = min(KEPT_PAIRS, pair_slots)
    more = max(pair_slots - kept, 1)
    layers, latents = lax.axis_size("layer"), lax.axis_size("latent")
    layer, latent = lax.axis_index("layer"), lax.axis_index("latent")
    core = latent % 2
    rows = tok_rows // 2
    chips = latents // 2
    width = model_width // chips
    column = (latent // 2) * width

    gain = part(out_gain, column, width, 1)
    target = part(part(targets[0], core * rows, rows, 0), column, width, 1)
    terms, left = [], gain
    for _ in range(3):
        terms.append(lax.reduce_precision(left, 8, 7))
        left = left - terms[-1]
    beside = jnp.concatenate([target, *[term.astype(BF16) for term in terms], jnp.zeros((13, width), BF16)], axis=0)
    layer_bits = [1 << s for s in range((layers - 1).bit_length())]
    chip_bits = [1 << s for s in range((chips - 1).bit_length(), 0, -1)]

    dec_hbm = in_hbm(dec_weight[0])
    vmem = pl.BlockSpec(memory_space=pltpu.VMEM)
    smem = pl.BlockSpec(memory_space=pltpu.SMEM)
    anyw = pl.BlockSpec(memory_space=pl.ANY)
    keep, send, ids = pl.pallas_call(
        encode_decode,
        out_shape=(
            pltpu.VMEM((rows, model_width), F32),
            pltpu.VMEM((rows, model_width), BF16),
            pltpu.SMEM((1, blocks + 1), jnp.int32),
        ),
        in_specs=[anyw, smem, anyw, anyw, anyw, anyw],
        out_specs=(vmem, vmem, smem),
        scratch_shapes=[
            pltpu.SMEM(block_list.shape, jnp.int32),
            pltpu.VMEM((tok_rows, model_width), BF16),
            pltpu.VMEM((1, local_latents), F32),
            pltpu.VMEM((pair_slots, model_width, PAIR), BF16),
            pltpu.VMEM((pair_slots, PAIR, model_width), BF16),
            pltpu.VMEM((2, tok_rows, PAIR), BF16),
            pltpu.VMEM((tok_rows, model_width), F32),
            pltpu.SemaphoreType.DMA((3,)),
            pltpu.SemaphoreType.DMA((blocks,)),
            pltpu.SemaphoreType.DMA((blocks,)),
        ],
        compiler_params=pltpu.CompilerParams(vmem_limit_bytes=32 << 20),
        name="encode_decode",
    )(in_hbm(block_list), block_count, in_hbm(residuals[0]), in_hbm(enc_bias), in_hbm(enc_weight[0]), dec_hbm)

    held = keep + swap(send, "latent", 1).astype(F32)
    for bit in chip_bits:
        half = held.shape[1] // 2
        upper = (latent & bit) != 0
        away = jnp.where(upper, held[:, :half], held[:, half:]).astype(BF16)
        mine = jnp.where(upper, held[:, half:], held[:, :half])
        if bit == chip_bits[-1]:
            away, beside = lax.optimization_barrier((away, beside))
            beside = swap(beside, "layer", 1)
        held = mine + swap(away, "latent", bit).astype(F32)
    own = held
    near = swap(own.astype(BF16), "layer", 1).astype(F32)
    near_target = beside[:rows]
    near_gain = sum(beside[rows + i : rows + i + 1].astype(F32) for i in range(3))
    square = gain * gain
    near_square = near_gain * near_gain
    all_square = square + near_square

    low = (layer & 1) == 0
    own_error = square * own - gain * target.astype(F32)
    near_error = near_square * near - near_gain * near_target.astype(F32)
    before = jnp.where(low, own, own + near)
    after = jnp.where(low, own_error + near_square * own + near_error, own_error + square * near)
    after_square = jnp.where(low, square + near_square, square)
    all_before = own + near
    all_after = own_error + near_error + jnp.where(low, near_square * own, square * near)
    for step in layer_bits[1:]:
        low = (layer & step) == 0
        there_square = swap(all_square, "layer", step)
        if step == layer_bits[-1]:
            got = swap(jnp.where(low, all_before, all_after).astype(BF16), "layer", step)
            break
        there_before = swap(all_before.astype(BF16), "layer", step).astype(F32)
        there_after = swap(all_after.astype(BF16), "layer", step).astype(F32)
        before, after = (
            jnp.where(low, before, before + there_before),
            jnp.where(low, after + there_square * all_before + there_after, after + after_square * there_before),
        )
        after_square = jnp.where(low, after_square + there_square, after_square)
        all_before, all_after = (
            all_before + there_before,
            all_after + there_after + jnp.where(low, there_square * all_before, all_square * there_before),
        )
        all_square = all_square + there_square

    columns = width // 2
    message, stay, send = pl.pallas_call(
        finish,
        out_shape=(
            pltpu.VMEM((rows, width + BLOCK), BF16),
            pltpu.VMEM((rows, columns), BF16),
            pltpu.VMEM((rows, columns), BF16),
        ),
        in_specs=[vmem] * 8,
        out_specs=(vmem, vmem, vmem),
        compiler_params=pltpu.CompilerParams(vmem_limit_bytes=16 << 20),
        name="finish",
    )(got, before, after, all_before, there_square, after_square, gain, target)

    for bit in reversed(chip_bits[1:]):
        upper = (latent & bit) != 0
        got = swap(message, "latent", bit)
        cut = message.shape[1] - BLOCK
        here, there = message[:, :cut], got[:, :cut]
        squares = (message[:, cut:].astype(F32) + got[:, cut:].astype(F32)).astype(BF16)
        message = jnp.concatenate([jnp.where(upper, there, here), jnp.where(upper, here, there), squares], axis=1)
    top, cut = chip_bits[0], model_width // 2
    got = swap(message, "latent", top)
    near = swap(jnp.concatenate([message, send], axis=1), "latent", 1)
    near_part, far_kept = pl.pallas_call(
        functools.partial(near_gradient, top),
        out_shape=(pltpu.VMEM((pair_slots, tok_rows, PAIR), F32), pltpu.VMEM((kept, PAIR, cut), BF16)),
        in_specs=[smem, vmem, vmem, anyw],
        out_specs=(vmem, vmem),
        scratch_shapes=[
            pltpu.VMEM((tok_rows, cut), BF16),
            pltpu.VMEM((pair_slots, PAIR, cut), BF16),
            pltpu.SemaphoreType.DMA((blocks,)),
            pltpu.SemaphoreType.DMA((blocks,)),
        ],
        compiler_params=pltpu.CompilerParams(vmem_limit_bytes=24 << 20),
        cost_estimate=pl.CostEstimate(flops=2 * tok_rows * cut * local_latents, bytes_accessed=2 * local_latents * model_width, transcendentals=0),
        name="near_gradient",
    )(ids, message, near, dec_hbm)
    got, near_part = lax.optimization_barrier((got, near_part))
    far = swap(got, "latent", 1)

    code_grad, recon, loss = pl.pallas_call(
        functools.partial(code_gradient, top),
        out_shape=(
            jax.ShapeDtypeStruct((tok_rows, local_latents), BF16),
            jax.ShapeDtypeStruct((columns, tok_rows), BF16),
            jax.ShapeDtypeStruct((1, 1), F32),
        ),
        in_specs=[smem] + [vmem] * 7 + [anyw],
        out_specs=(vmem, vmem, vmem),
        scratch_shapes=[
            pltpu.VMEM((tok_rows, cut), BF16),
            pltpu.VMEM((tok_rows, columns), F32),
            pltpu.VMEM((more, PAIR, cut), BF16),
            pltpu.SemaphoreType.DMA((blocks,)),
        ],
        compiler_params=pltpu.CompilerParams(vmem_limit_bytes=16 << 20),
        name="code_gradient",
    )(ids, message, near, got, far, stay, *[pltpu.with_memory_space_constraint(a, pltpu.VMEM) for a in (near_part, far_kept)], dec_hbm)
    return recon.T[None], code_grad[None], loss


def solution(mesh):
    placed = (
        P("layer", "groups", None),
        P("layer", "groups", None),
        P("layer", None, "latent"),
        P("layer", "latent"),
        P("layer", "latent", None),
        P("layer", None),
        P("layer", "groups", None),
        P("layer", "groups"),
    )
    return jax.shard_map(
        local,
        mesh=mesh,
        in_specs=placed,
        out_specs=(
            P("layer", "groups", "latent"),
            P("layer", "groups", "latent"),
            P("groups", "layer"),
        ),
        check_vma=False,
    )
```

time: 57.7 us -> 42.8 us (0.74)
  the two profiles are of different devices: /device:TPU:1 before, /device:TPU:0 now
where the time goes in v3:
time: 42.8 us; the launch traced here: 42 us
  waiting for transfers between devices  20.5 us (48%)
  Pallas kernels  11.8 us (28%)
  starting transfers between devices  7.26 us (17%)
  between operations  1.48 us (3%)
  other arithmetic  0.54 us (1%)
  local copies, waits for them, and re-layouts  0.46 us (1%)
    ppermute x9, waiting for transfers between devices, swap(): return lax.ppermute(value, axis, [(i, i ^ bit) for i in range(size)])  20.5 us
    ppermute x9, starting transfers between devices, swap(): return lax.ppermute(value, axis, [(i, i ^ bit) for i in range(size)])  7.26 us
    pallas_call x1, Pallas kernels, local(): pl.pallas_call(encode_decode, out_shape=(pltpu.VMEM((rows, model_width),...  6.41 us
    pallas_call x1, Pallas kernels, local(): pl.pallas_call(functools.partial(near_gradient, top), out_shape=(pltpu.VM...  2.69 us
    pallas_call x1, Pallas kernels, local(): pl.pallas_call(functools.partial(code_gradient, top), out_shape=(jax.Shap...  2.42 us
  transfers between devices with their start and end apart: 9, of which 8 were waited for; matrix products, arithmetic and copies ran while one was open for 1% of the time, Pallas kernels for 6%

profile of v3, /device:TPU:0, one launch (start us, length us, event | category | flops | bytes accessed | tf_op | source)
XLA Modules:
  0.0 42.0 jit_solution(3742845452081704797)
XLA Ops:
  1.3 6.4 %encode_decode.1 = (f32[64,2304]{1,0:T(8,128)S(1)}, bf16[64,2304]{1,0:T(8,128)(2,1)S(1)}, s32[1,17]{1,0:T(1,128)S(4)}) custom-call(s32[1,1,24]{2,1,0:T(1,128)} %list_any.1, s32[1,1]{1,0:T(1,128)S(6)} %copy.11.count_ref, bf16[128,2304]{1,0:T(8,128)(2,1)} %bitcast.15, f32[1,2048]{1,0:T(1,128)} %bias_any.1, bf16[2304,2048]{1,0:T(8,128)(2,1)} %bitcast.14, ...), custom_call_target="tpu_custom_call" | custom-call | tf_op jit(solution)/shard_map/encode_decode/pallas_call | solution.py:277
  7.7 0.1 collective-permute-start
  7.9 0.1 dynamic-slice_bitcast_fusion.target_ref
  8.1 0.3 concatenate.6
  8.4 1.0 %collective-permute-done = bf16[64,2304]{1,0:T(8,128)(2,1)S(1)} collective-permute-done((bf16[64,2304]{1,0:T(8,128)(2,1)S(1)}, bf16[64,2304]{1,0:T(8,128)(2,1)S(1)}, u32[]{:S(2)}, u32[]{:S(2)}) %collective-permute-start) | collective-permute-done | bytes 294944 | tf_op jit(solution)/shard_map/ppermute | solution.py:237
  9.4 0.1 convert_add_fusion
  9.5 3.1 %collective-permute-start.1 = (bf16[64,1152]{1,0:T(8,128)(2,1)S(1)}, bf16[64,1152]{1,0:T(8,128)(2,1)S(1)}, u32[]{:S(2)}, u32[]{:S(2)}) collective-permute-start(bf16[64,1152]{1,0:T(8,128)(2,1)S(1)} %select_convert_fusion), channel_id=1, source_target_pairs={{0,2},{1,3},{2,0},{3,1},{4,6},{5,7},{6,4},{7,5},{8,10},{9,11},{10,... | collective-permute-start | bytes 442376 | tf_op jit(solution)/shard_map/ppermute | solution.py:237
  12.5 4.1 %collective-permute-done.1 = bf16[64,1152]{1,0:T(8,128)(2,1)S(1)} collective-permute-done((bf16[64,1152]{1,0:T(8,128)(2,1)S(1)}, bf16[64,1152]{1,0:T(8,128)(2,1)S(1)}, u32[]{:S(2)}, u32[]{:S(2)}) %collective-permute-start.1) | collective-permute-done | bytes 147488 | tf_op jit(solution)/shard_map/ppermute | solution.py:237
  16.7 0.1 fusion.12
  16.7 0.1 collective-permute-start.2
  16.8 2.1 %collective-permute-done.3 = bf16[80,1152]{1,0:T(8,128)(2,1)S(1)} collective-permute-done((bf16[80,1152]{1,0:T(8,128)(2,1)S(1)}, bf16[80,1152]{1,0:T(8,128)(2,1)S(1)}, u32[]{:S(2)}, u32[]{:S(2)}) %collective-permute-start.3) | collective-permute-done | bytes 184352 | tf_op jit(solution)/shard_map/ppermute | solution.py:237
  19.0 3.2 %collective-permute-done.2 = bf16[64,1152]{1,0:T(8,128)(2,1)S(1)} collective-permute-done((bf16[64,1152]{1,0:T(8,128)(2,1)S(1)}, bf16[64,1152]{1,0:T(8,128)(2,1)S(1)}, u32[]{:S(2)}, u32[]{:S(2)}) %collective-permute-start.2) | collective-permute-done | bytes 147488 | tf_op jit(solution)/shard_map/ppermute | solution.py:237
  22.2 0.3 fusion.5
  22.4 0.7 %collective-permute-start.4 = (bf16[64,1152]{1,0:T(8,128)(2,1)S(1)}, bf16[64,1152]{1,0:T(8,128)(2,1)S(1)}, u32[]{:S(2)}, u32[]{:S(2)}) collective-permute-start(bf16[64,1152]{1,0:T(8,128)(2,1)S(1)} %get-tuple-element.43), channel_id=1, source_target_pairs={{0,8},{4,12},{8,0},{12,4},{1,9},{5,13},{9,1},{13,5},{2,10},{6,14},... | collective-permute-start | bytes 442376 | tf_op jit(solution)/shard_map/ppermute | solution.py:237
  23.2 2.3 %collective-permute-start.5 = (f32[1,1152]{1,0:T(1,128)S(1)}, f32[1,1152]{1,0:T(1,128)S(1)}, u32[]{:S(2)}, u32[]{:S(2)}) collective-permute-start(f32[1,1152]{1,0:T(1,128)S(1)} %get-tuple-element.46), channel_id=1, source_target_pairs={{0,8},{4,12},{8,0},{12,4},{1,9},{5,13},{9,1},{13,5},{2,10},{6,14},... | collective-permute-start | bytes 13832 | tf_op jit(solution)/shard_map/ppermute | solution.py:237
  25.4 5.8 %collective-permute-done.5.there_square_ref = f32[1,1152]{1,0:T(1,128)S(1)} collective-permute-done((f32[1,1152]{1,0:T(1,128)S(1)}, f32[1,1152]{1,0:T(1,128)S(1)}, u32[]{:S(2)}, u32[]{:S(2)}) %collective-permute-start.5) | collective-permute-done | bytes 4640 | tf_op jit(solution)/shard_map/ppermute | solution.py:237
  31.2 0.2 finish.1
  31.5 0.1 collective-permute-start.6
  31.6 1.0 %collective-permute-start.7 = (bf16[64,1280]{1,0:T(8,128)(2,1)S(1)}, bf16[64,1280]{1,0:T(8,128)(2,1)S(1)}, u32[]{:S(2)}, u32[]{:S(2)}) collective-permute-start(bf16[64,1280]{1,0:T(8,128)(2,1)S(1)} %get-tuple-element.23.own_ref), channel_id=1, source_target_pairs={{0,2},{1,3},{2,0},{3,1},{4,6},{5,7},{6,4},{7,5},{8,10},{9,11},{10,... | collective-permute-start | bytes 491528 | tf_op jit(solution)/shard_map/ppermute | solution.py:237
  32.6 0.5 %collective-permute-done.6.near_ref = bf16[64,1856]{1,0:T(8,128)(2,1)S(1)} collective-permute-done((bf16[64,1856]{1,0:T(8,128)(2,1)S(1)}, bf16[64,1856]{1,0:T(8,128)(2,1)S(1)}, u32[]{:S(2)}, u32[]{:S(2)}) %collective-permute-start.6) | collective-permute-done | bytes 237600 | tf_op jit(solution)/shard_map/ppermute | solution.py:237
  33.1 2.7 %near_gradient.1 = (f32[8,128,256]{2,1,0:T(8,128)S(1)}, bf16[3,256,1152]{2,1,0:T(8,128)(2,1)S(1)}) custom-call(s32[1,17]{1,0:T(1,128)S(4)} %get-tuple-element.18.ids_ref, bf16[64,1280]{1,0:T(8,128)(2,1)S(1)} %get-tuple-element.23.own_ref, bf16[64,1856]{1,0:T(8,128)(2,1)S(1)} %collective-permute-done.6.near_ref, bf16[2048,2304]{1,0:T(8,128)(2,1)} %bitcast.12), custom_call_target="tpu_custom_call" | custom-call | flops 603979776 | bytes 9437184 | tf_op jit(solution)/shard_map/near_gradient/pallas_call | solution.py:371
  35.8 2.4 %collective-permute-done.7.got_ref = bf16[64,1280]{1,0:T(8,128)(2,1)S(1)} collective-permute-done((bf16[64,1280]{1,0:T(8,128)(2,1)S(1)}, bf16[64,1280]{1,0:T(8,128)(2,1)S(1)}, u32[]{:S(2)}, u32[]{:S(2)}) %collective-permute-start.7) | collective-permute-done | bytes 163872 | tf_op jit(solution)/shard_map/ppermute | solution.py:237
  38.2 1.4 %collective-permute-done.8.far_ref = bf16[64,1280]{1,0:T(8,128)(2,1)S(1)} collective-permute-done((bf16[64,1280]{1,0:T(8,128)(2,1)S(1)}, bf16[64,1280]{1,0:T(8,128)(2,1)S(1)}, u32[]{:S(2)}, u32[]{:S(2)}) %collective-permute-start.8) | collective-permute-done | bytes 163872 | tf_op jit(solution)/shard_map/ppermute | solution.py:237
  39.6 2.4 %code_gradient.1 = (bf16[128,2048]{1,0:T(8,128)(2,1)}, bf16[576,128]{1,0:T(8,128)(2,1)}, f32[1,1]{1,0:T(1,128)}) custom-call(s32[1,17]{1,0:T(1,128)S(4)} %get-tuple-element.18.ids_ref, bf16[64,1280]{1,0:T(8,128)(2,1)S(1)} %get-tuple-element.23.own_ref, bf16[64,1856]{1,0:T(8,128)(2,1)S(1)} %collective-permute-done.6.near_ref, ...), custom_call_target="tpu_custom_call" | custom-call | tf_op jit(solution)/shard_map/code_gradient/pallas_call | solution.py:389
  (14 shorter events, 0.2 us)
Async XLA Ops:
  1.3 6.5 %copy-start.1 = (f32[1,2304]{1,0:T(1,128)S(1)}, f32[1,2304]{1,0:T(1,128)}, u32[]{:S(2)}) copy-start(f32[1,2304]{1,0:T(1,128)} %param.13) | copy-start | bytes 27652
  1.3 6.6 %copy-start = (bf16[1,128,2304]{2,1,0:T(8,128)(2,1)S(1)}, bf16[1,128,2304]{2,1,0:T(8,128)(2,1)}, u32[]{:S(2)}) copy-start(bf16[1,128,2304]{2,1,0:T(8,128)(2,1)} %param.9) | copy-start | bytes 1769476
  7.7 1.6 %collective-permute-start = (bf16[64,2304]{1,0:T(8,128)(2,1)S(1)}, bf16[64,2304]{1,0:T(8,128)(2,1)S(1)}, u32[]{:S(2)}, u32[]{:S(2)}) collective-permute-start(bf16[64,2304]{1,0:T(8,128)(2,1)S(1)} %get-tuple-element.20), channel_id=1, source_target_pairs={{0,1},{1,0},{2,3},{3,2},{4,5},{5,4},{6,7},{7,6},{8,9},{9,8},{10,11... | collective-permute-start | bytes 884744 | tf_op jit(solution)/shard_map/ppermute | solution.py:237
  9.5 7.2 %collective-permute-start.1 = (bf16[64,1152]{1,0:T(8,128)(2,1)S(1)}, bf16[64,1152]{1,0:T(8,128)(2,1)S(1)}, u32[]{:S(2)}, u32[]{:S(2)}) collective-permute-start(bf16[64,1152]{1,0:T(8,128)(2,1)S(1)} %select_convert_fusion), channel_id=1, source_target_pairs={{0,2},{1,3},{2,0},{3,1},{4,6},{5,7},{6,4},{7,5},{8,10},{9,11},{10,... | collective-permute-start | bytes 442376 | tf_op jit(solution)/shard_map/ppermute | solution.py:237
  12.5 6.4 %collective-permute-start.3 = (bf16[80,1152]{1,0:T(8,128)(2,1)S(1)}, bf16[80,1152]{1,0:T(8,128)(2,1)S(1)}, u32[]{:S(2)}, u32[]{:S(2)}) collective-permute-start(bf16[80,1152]{1,0:T(8,128)(2,1)S(1)} %concatenate.6), channel_id=1, source_target_pairs={{0,4},{4,0},{8,12},{12,8},{1,5},{5,1},{9,13},{13,9},{2,6},{6,2},{1... | collective-permute-start | bytes 552968 | tf_op jit(solution)/shard_map/ppermute | solution.py:237
  16.7 5.4 %collective-permute-start.2 = (bf16[64,1152]{1,0:T(8,128)(2,1)S(1)}, bf16[64,1152]{1,0:T(8,128)(2,1)S(1)}, u32[]{:S(2)}, u32[]{:S(2)}) collective-permute-start(bf16[64,1152]{1,0:T(8,128)(2,1)S(1)} %get-tuple-element.40), channel_id=1, source_target_pairs={{0,4},{4,0},{8,12},{12,8},{1,5},{5,1},{9,13},{13,9},{2,6},{6,2},{1... | collective-permute-start | bytes 442376 | tf_op jit(solution)/shard_map/ppermute | solution.py:237
  22.4 8.8 %collective-permute-start.4 = (bf16[64,1152]{1,0:T(8,128)(2,1)S(1)}, bf16[64,1152]{1,0:T(8,128)(2,1)S(1)}, u32[]{:S(2)}, u32[]{:S(2)}) collective-permute-start(bf16[64,1152]{1,0:T(8,128)(2,1)S(1)} %get-tuple-element.43), channel_id=1, source_target_pairs={{0,8},{4,12},{8,0},{12,4},{1,9},{5,13},{9,1},{13,5},{2,10},{6,14},... | collective-permute-start | bytes 442376 | tf_op jit(solution)/shard_map/ppermute | solution.py:237
  23.2 8.1 %collective-permute-start.5 = (f32[1,1152]{1,0:T(1,128)S(1)}, f32[1,1152]{1,0:T(1,128)S(1)}, u32[]{:S(2)}, u32[]{:S(2)}) collective-permute-start(f32[1,1152]{1,0:T(1,128)S(1)} %get-tuple-element.46), channel_id=1, source_target_pairs={{0,8},{4,12},{8,0},{12,4},{1,9},{5,13},{9,1},{13,5},{2,10},{6,14},... | collective-permute-start | bytes 13832 | tf_op jit(solution)/shard_map/ppermute | solution.py:237
  31.5 1.6 %collective-permute-start.6 = (bf16[64,1856]{1,0:T(8,128)(2,1)S(1)}, bf16[64,1856]{1,0:T(8,128)(2,1)S(1)}, u32[]{:S(2)}, u32[]{:S(2)}) collective-permute-start(bf16[64,1856]{1,0:T(8,128)(2,1)S(1)} %pad_maximum_fusion), channel_id=1, source_target_pairs={{0,1},{1,0},{2,3},{3,2},{4,5},{5,4},{6,7},{7,6},{8,9},{9,8},{10,11... | collective-permute-start | bytes 712712 | tf_op jit(solution)/shard_map/ppermute | solution.py:237
  31.6 6.6 %collective-permute-start.7 = (bf16[64,1280]{1,0:T(8,128)(2,1)S(1)}, bf16[64,1280]{1,0:T(8,128)(2,1)S(1)}, u32[]{:S(2)}, u32[]{:S(2)}) collective-permute-start(bf16[64,1280]{1,0:T(8,128)(2,1)S(1)} %get-tuple-element.23.own_ref), channel_id=1, source_target_pairs={{0,2},{1,3},{2,0},{3,1},{4,6},{5,7},{6,4},{7,5},{8,10},{9,11},{10,... | collective-permute-start | bytes 491528 | tf_op jit(solution)/shard_map/ppermute | solution.py:237
  38.2 1.4 %collective-permute-start.8 = (bf16[64,1280]{1,0:T(8,128)(2,1)S(1)}, bf16[64,1280]{1,0:T(8,128)(2,1)S(1)}, u32[]{:S(2)}, u32[]{:S(2)}) collective-permute-start(bf16[64,1280]{1,0:T(8,128)(2,1)S(1)} %collective-permute-done.7.got_ref), channel_id=1, source_target_pairs={{0,1},{1,0},{2,3},{3,2},{4,5},{5,4},{6,7},{7,6},{8,9},{9,8},{10,11... | collective-permute-start | bytes 491528 | tf_op jit(solution)/shard_map/ppermute | solution.py:237

commit v4 on v3

--- a/solution.py
+++ b/solution.py
@@ -26,17 +26,24 @@
         load.start()
     where = lax.axis_index("latent")
     first = where * blocks
-    slots = list_ref.shape[2]
+    total[...] = jnp.zeros_like(total)
+
+    def place_of(n):
+        return lax.div(n, 4), pl.ds(pl.multiple_of(lax.rem(n, 4) * BLOCK, BLOCK), BLOCK)
+
+    def rows_of(n):
+        return pl.ds(pl.multiple_of(ids_ref[0, n] * BLOCK, BLOCK), BLOCK)
+
+    def enc_copy(n):
+        quad, place = place_of(n)
+        return pltpu.make_async_copy(enc_ref.at[:, rows_of(n)], enc_held.at[quad, :, place], enc_sem.at[n])
+
+    def dec_copy(n):
+        quad, place = place_of(n)
+        return pltpu.make_async_copy(dec_ref.at[rows_of(n), :], dec_held.at[quad, place, :], dec_sem.at[n])
+
+    list_load.wait()
     count = count_ref[0, 0]
-    total[...] = jnp.zeros_like(total)
-
-    def copies(block, n):
-        pair, half = lax.div(n, 2), pl.multiple_of(lax.rem(n, 2) * BLOCK, BLOCK)
-        source = pl.ds(pl.multiple_of(block * BLOCK, BLOCK), BLOCK)
-        return (
-            pltpu.make_async_copy(enc_ref.at[:, source], enc_held.at[pair, :, pl.ds(half, BLOCK)], enc_sem.at[n]),
-            pltpu.make_async_copy(dec_ref.at[source, :], dec_held.at[pair, pl.ds(half, BLOCK), :], dec_sem.at[n]),
-        )
 
     def look(slot, n):
         block = list_ref[0, 0, slot] - first
@@ -45,59 +52,50 @@
         @pl.when(live)
         def _():
             ids_ref[0, n] = block
-            for copy in copies(block, n):
-                copy.start()
+            enc_copy(n).start()
 
         return n + live.astype(jnp.int32)
 
-    list_load.wait()
-    live_count = lax.fori_loop(0, slots, look, jnp.int32(0))
+    live_count = lax.fori_loop(0, jnp.minimum(count, list_ref.shape[2]), look, jnp.int32(0))
     ids_ref[0, blocks] = live_count
-    pairs = lax.div(live_count + 1, 2)
-
-    @pl.when(lax.rem(live_count, 2) == 1)
-    def _():
-        dec_held[pairs - 1, pl.ds(BLOCK, BLOCK), :] = jnp.zeros((BLOCK, dec_held.shape[2]), BF16)
-        ids_ref[0, live_count] = ids_ref[0, live_count - 1]
-
+    lax.fori_loop(0, live_count, lambda n, c: (dec_copy(n).start(), c)[1], 0)
+    quads = lax.div(live_count + 1, 4)
+    last_pair = (lax.rem(live_count, 4) == 1) | (lax.rem(live_count, 4) == 2)
+
+    def clear(n, carry):
+        quad, place = place_of(n)
+        dec_held[quad, place, :] = jnp.zeros((BLOCK, dec_held.shape[2]), BF16)
+        ids_ref[0, n] = ids_ref[0, 0]
+        return carry
+
+    lax.fori_loop(live_count, jnp.where(last_pair, 4 * quads + 2, 4 * quads), clear, 0)
     for load in loads:
         load.wait()
 
-    def arrive(pair, which):
-        n = 2 * pair
-        copies(ids_ref[0, n], n)[which].wait()
-
-        @pl.when(n + 1 < live_count)
-        def _():
-            copies(ids_ref[0, n + 1], n + 1)[which].wait()
-
-    def encode(pair):
-        n = 2 * pair
-        bias = jnp.concatenate(
-            [bias_ref[:, pl.ds(pl.multiple_of(ids_ref[0, i] * BLOCK, BLOCK), BLOCK)] for i in (n, n + 1)], axis=1
-        )
-        pre_act = jnp.dot(x_ref[...], enc_held[pair], preferred_element_type=F32) + bias
+    def arrive(copy, quad, size):
+        for i in range(size):
+            n = 4 * quad + i
+            pl.when(n < live_count)(lambda n=n: copy(n).wait())
+
+    def encode(quad, size):
+        arrive(enc_copy, quad, size)
+        lanes = pl.ds(0, size * BLOCK)
+        bias = jnp.concatenate([bias_ref[:, rows_of(4 * quad + i)] for i in range(size)], axis=1)
+        pre_act = jnp.dot(x_ref[...], enc_held[quad, :, lanes], preferred_element_type=F32) + bias
         lane = lax.broadcasted_iota(jnp.int32, pre_act.shape, 1)
-        used = (lane < BLOCK) | (n + 1 < live_count)
-        codes[lax.rem(pair, 2)] = jnp.where(used, jnp.maximum(pre_act, 0.0), 0.0).astype(BF16)
-
-    def decode(pair):
-        total[...] += jnp.dot(codes[lax.rem(pair, 2)], dec_held[pair], preferred_element_type=F32)
-
-    def step(pair, carry):
-        arrive(pair, 0)
-        arrive(pair - 1, 1)
-        encode(pair)
-        decode(pair - 1)
+        used = lane < (live_count - 4 * quad) * BLOCK
+        codes[quad, :, lanes] = jnp.where(used, jnp.maximum(pre_act, 0.0), 0.0).astype(BF16)
+
+    def decode(pair, carry):
+        quad, lanes = lax.div(pair, 2), pl.ds(pl.multiple_of(lax.rem(pair, 2) * PAIR, PAIR), PAIR)
+        for n in (2 * pair, 2 * pair + 1):
+            pl.when(n < live_count)(lambda n=n: dec_copy(n).wait())
+        total[...] += jnp.dot(codes[quad, :, lanes], dec_held[quad, lanes, :], preferred_element_type=F32)
         return carry
 
-    @pl.when(pairs > 0)
-    def _():
-        arrive(0, 0)
-        encode(0)
-        lax.fori_loop(1, pairs, step, 0)
-        arrive(pairs - 1, 1)
-        decode(pairs - 1)
+    lax.fori_loop(0, quads, lambda quad, c: (encode(quad, 4), c)[1], 0)
+    pl.when(last_pair)(lambda: encode(quads, 2))
+    lax.fori_loop(0, lax.div(live_count + 1, 2), decode, 0)
 
     rows = keep_ref.shape[0]
     core = lax.rem(where, 2)
@@ -184,7 +182,7 @@
 
 
 def code_gradient(
-    top, ids_ref, own_ref, near_ref, got_ref, far_ref, stay_ref, part_ref, far_kept, dec_ref,
+    top, ids_ref, own_ref, got_ref, far_ref, stay_ref, other_ref, part_ref, far_kept, dec_ref,
     out_ref, recon_ref, mean_ref, grad, fitted, dec_far, far_sem,
 ):
     blocks = far_sem.shape[0]
@@ -225,9 +223,9 @@
     lax.fori_loop(0, jnp.minimum(pairs, kept), step, 0)
     lax.fori_loop(kept, pairs, fetched, 0)
     columns = stay_ref.shape[1]
-    by_core(core, stay_ref[...].astype(F32), near_ref[:, cut + BLOCK :].astype(F32), fitted)
+    by_core(core, stay_ref[...].astype(F32), other_ref[:, :columns].astype(F32), fitted)
     recon_ref[...] = jnp.transpose(fitted[...]).astype(BF16)
-    squares = sum(ref[:, cut : cut + BLOCK].astype(F32) for ref in (own_ref, near_ref, got_ref, far_ref))
+    squares = sum(ref[:, cut:].astype(F32) for ref in (own_ref, got_ref, far_ref)) + other_ref[:, columns:].astype(F32)
     total = jnp.sum(jnp.sum(squares, axis=0, keepdims=True), axis=1, keepdims=True)
     mean_ref[...] = total / (grad.shape[0] * 2 * cut)
 
@@ -243,6 +241,41 @@
 
 def part(value, start, size, axis):
     return lax.dynamic_slice_in_dim(value, start, size, axis)
+
+
+def encode_call(block_list, block_count, x, bias, enc, dec):
+    tok_rows, model_width = x.shape
+    local_latents = enc.shape[1]
+    blocks = local_latents // BLOCK
+    quad_slots = (blocks + 3) // 4
+    rows = tok_rows // 2
+    vmem = pl.BlockSpec(memory_space=pltpu.VMEM)
+    smem = pl.BlockSpec(memory_space=pltpu.SMEM)
+    anyw = pl.BlockSpec(memory_space=pl.ANY)
+    return pl.pallas_call(
+        encode_decode,
+        out_shape=(
+            pltpu.VMEM((rows, model_width), F32),
+            pltpu.VMEM((rows, model_width), BF16),
+            pltpu.SMEM((1, blocks + 1), jnp.int32),
+        ),
+        in_specs=[anyw, smem, anyw, anyw, anyw, anyw],
+        out_specs=(vmem, vmem, smem),
+        scratch_shapes=[
+            pltpu.SMEM(block_list.shape, jnp.int32),
+            pltpu.VMEM((tok_rows, model_width), BF16),
+            pltpu.VMEM((1, local_latents), F32),
+            pltpu.VMEM((quad_slots, model_width, 4 * BLOCK), BF16),
+            pltpu.VMEM((quad_slots, 4 * BLOCK, model_width), BF16),
+            pltpu.VMEM((quad_slots, tok_rows, 4 * BLOCK), BF16),
+            pltpu.VMEM((tok_rows, model_width), F32),
+            pltpu.SemaphoreType.DMA((3,)),
+            pltpu.SemaphoreType.DMA((blocks,)),
+            pltpu.SemaphoreType.DMA((blocks,)),
+        ],
+        compiler_params=pltpu.CompilerParams(vmem_limit_bytes=32 << 20),
+        name="encode_decode",
+    )(block_list, block_count, x, bias, enc, dec)
 
 
 def local(residuals, targets, enc_weight, enc_bias, dec_weight, out_gain, block_list, block_count):
@@ -274,30 +307,9 @@
     vmem = pl.BlockSpec(memory_space=pltpu.VMEM)
     smem = pl.BlockSpec(memory_space=pltpu.SMEM)
     anyw = pl.BlockSpec(memory_space=pl.ANY)
-    keep, send, ids = pl.pallas_call(
-        encode_decode,
-        out_shape=(
-            pltpu.VMEM((rows, model_width), F32),
-            pltpu.VMEM((rows, model_width), BF16),
-            pltpu.SMEM((1, blocks + 1), jnp.int32),
-        ),
-        in_specs=[anyw, smem, anyw, anyw, anyw, anyw],
-        out_specs=(vmem, vmem, smem),
-        scratch_shapes=[
-            pltpu.SMEM(block_list.shape, jnp.int32),
-            pltpu.VMEM((tok_rows, model_width), BF16),
-            pltpu.VMEM((1, local_latents), F32),
-            pltpu.VMEM((pair_slots, model_width, PAIR), BF16),
-            pltpu.VMEM((pair_slots, PAIR, model_width), BF16),
-            pltpu.VMEM((2, tok_rows, PAIR), BF16),
-            pltpu.VMEM((tok_rows, model_width), F32),
-            pltpu.SemaphoreType.DMA((3,)),
-            pltpu.SemaphoreType.DMA((blocks,)),
-            pltpu.SemaphoreType.DMA((blocks,)),
-        ],
-        compiler_params=pltpu.CompilerParams(vmem_limit_bytes=32 << 20),
-        name="encode_decode",
-    )(in_hbm(block_list), block_count, in_hbm(residuals[0]), in_hbm(enc_bias), in_hbm(enc_weight[0]), dec_hbm)
+    keep, send, ids = encode_call(
+        in_hbm(block_list), block_count, in_hbm(residuals[0]), in_hbm(enc_bias), in_hbm(enc_weight[0]), dec_hbm
+    )
 
     held = keep + swap(send, "latent", 1).astype(F32)
     for bit in chip_bits:
@@ -306,7 +318,6 @@
         away = jnp.where(upper, held[:, :half], held[:, half:]).astype(BF16)
         mine = jnp.where(upper, held[:, half:], held[:, :half])
         if bit == chip_bits[-1]:
-            away, beside = lax.optimization_barrier((away, beside))
             beside = swap(beside, "layer", 1)
         held = mine + swap(away, "latent", bit).astype(F32)
     own = held
@@ -367,7 +378,8 @@
         message = jnp.concatenate([jnp.where(upper, there, here), jnp.where(upper, here, there), squares], axis=1)
     top, cut = chip_bits[0], model_width // 2
     got = swap(message, "latent", top)
-    near = swap(jnp.concatenate([message, send], axis=1), "latent", 1)
+    near = swap(message[:, :cut], "latent", 1)
+    send = jnp.concatenate([send, message[:, cut:]], axis=1)
     near_part, far_kept = pl.pallas_call(
         functools.partial(near_gradient, top),
         out_shape=(pltpu.VMEM((pair_slots, tok_rows, PAIR), F32), pltpu.VMEM((kept, PAIR, cut), BF16)),
@@ -380,11 +392,11 @@
             pltpu.SemaphoreType.DMA((blocks,)),
         ],
         compiler_params=pltpu.CompilerParams(vmem_limit_bytes=24 << 20),
-        cost_estimate=pl.CostEstimate(flops=2 * tok_rows * cut * local_latents, bytes_accessed=2 * local_latents * model_width, transcendentals=0),
         name="near_gradient",
     )(ids, message, near, dec_hbm)
-    got, near_part = lax.optimization_barrier((got, near_part))
+    got, near_part, send = lax.optimization_barrier((got, near_part, send))
     far = swap(got, "latent", 1)
+    other = swap(send, "latent", 1)
 
     code_grad, recon, loss = pl.pallas_call(
         functools.partial(code_gradient, top),
@@ -403,7 +415,7 @@
         ],
         compiler_params=pltpu.CompilerParams(vmem_limit_bytes=16 << 20),
         name="code_gradient",
-    )(ids, message, near, got, far, stay, *[pltpu.with_memory_space_constraint(a, pltpu.VMEM) for a in (near_part, far_kept)], dec_hbm)
+    )(ids, message, got, far, stay, other, *[pltpu.with_memory_space_constraint(a, pltpu.VMEM) for a in (near_part, far_kept)], dec_hbm)
     return recon.T[None], code_grad[None], loss
 
 

time: 42.8 us -> 40.1 us (0.937); the launches traced: 42 us -> 40.4 us
  starting transfers between devices: 7.26 us -> 12.2 us
  waiting for transfers between devices: 20.5 us -> 16.1 us
  Pallas kernels: 11.8 us -> 9.51 us
    ppermute x9 -> x10, starting transfers between devices: 7.26 us -> 12.2 us  [swap(): return lax.ppermute(value, axis, [(i, i ^ bit) for i in range(size)])]
    ppermute x9 -> x10, waiting for transfers between devices: 20.5 us -> 16.1 us  [swap(): return lax.ppermute(value, axis, [(i, i ^ bit) for i in range(size)])]
    pallas_call x1, Pallas kernels: 6.41 us -> 4.8 us  [encode_call(): pl.pallas_call(encode_decode, out_shape=(pltpu.VMEM((rows, model_width),...]
  transfers between devices with their start and end apart: 9 -> 10, of which waited for: 8 -> 6; matrix products, arithmetic and copies ran while one was open for 1% -> 2% of each run, Pallas kernels for 6% -> 6%
where the time goes in v4:
time: 40.1 us; the launch traced here: 40.4 us
  waiting for transfers between devices  16.1 us (40%)
  starting transfers between devices  12.2 us (30%)
  Pallas kernels  9.51 us (24%)
  between operations  1.48 us (4%)
  other arithmetic  0.6 us (1%)
  local copies, waits for them, and re-layouts  0.48 us (1%)
    ppermute x10, waiting for transfers between devices, swap(): return lax.ppermute(value, axis, [(i, i ^ bit) for i in range(size)])  16.1 us
    ppermute x10, starting transfers between devices, swap(): return lax.ppermute(value, axis, [(i, i ^ bit) for i in range(size)])  12.2 us
    pallas_call x1, Pallas kernels, encode_call(): pl.pallas_call(encode_decode, out_shape=(pltpu.VMEM((rows, model_width),...  4.8 us
    pallas_call x1, Pallas kernels, local(): pl.pallas_call(functools.partial(near_gradient, top), out_shape=(pltpu.VM...  2.35 us
    pallas_call x1, Pallas kernels, local(): pl.pallas_call(functools.partial(code_gradient, top), out_shape=(jax.Shap...  2.12 us
  transfers between devices with their start and end apart: 10, of which 6 were waited for; matrix products, arithmetic and copies ran while one was open for 2% of the time, Pallas kernels for 6%

profile of v4, /device:TPU:0, one launch (start us, length us, event | category | flops | bytes accessed | tf_op | source)
XLA Modules:
  0.0 40.4 jit_solution(10527745702633181093)
XLA Ops:
  1.3 4.8 %encode_decode.1 = (f32[64,2304]{1,0:T(8,128)S(1)}, bf16[64,2304]{1,0:T(8,128)(2,1)S(1)}, s32[1,17]{1,0:T(1,128)S(4)}) custom-call(s32[1,1,24]{2,1,0:T(1,128)} %list_any.1, s32[1,1]{1,0:T(1,128)S(6)} %copy.11.count_ref, bf16[128,2304]{1,0:T(8,128)(2,1)} %bitcast.15, f32[1,2048]{1,0:T(1,128)} %bias_any.1, bf16[2304,2048]{1,0:T(8,128)(2,1)} %bitcast.14, ...), custom_call_target="tpu_custom_call" | custom-call | tf_op jit(solution)/shard_map/encode_decode/pallas_call | solution.py:255
  6.1 0.1 collective-permute-start
  6.3 0.1 dynamic-slice_bitcast_fusion.target_ref
  6.5 0.3 concatenate.6
  6.8 3.4 %collective-permute-start.3 = (bf16[80,1152]{1,0:T(8,128)(2,1)S(1)}, bf16[80,1152]{1,0:T(8,128)(2,1)S(1)}, u32[]{:S(2)}, u32[]{:S(2)}) collective-permute-start(bf16[80,1152]{1,0:T(8,128)(2,1)S(1)} %concatenate.6), channel_id=1, source_target_pairs={{0,4},{4,0},{8,12},{12,8},{1,5},{5,1},{9,13},{13,9},{2,6},{6,2},{1... | collective-permute-start | bytes 552968 | tf_op jit(solution)/shard_map/ppermute | solution.py:235
  10.3 2.0 %collective-permute-start.1 = (bf16[64,1152]{1,0:T(8,128)(2,1)S(1)}, bf16[64,1152]{1,0:T(8,128)(2,1)S(1)}, u32[]{:S(2)}, u32[]{:S(2)}) collective-permute-start(bf16[64,1152]{1,0:T(8,128)(2,1)S(1)} %select_convert_fusion), channel_id=1, source_target_pairs={{0,2},{1,3},{2,0},{3,1},{4,6},{5,7},{6,4},{7,5},{8,10},{9,11},{10,... | collective-permute-start | bytes 442376 | tf_op jit(solution)/shard_map/ppermute | solution.py:235
  12.3 2.8 %collective-permute-done.3 = bf16[80,1152]{1,0:T(8,128)(2,1)S(1)} collective-permute-done((bf16[80,1152]{1,0:T(8,128)(2,1)S(1)}, bf16[80,1152]{1,0:T(8,128)(2,1)S(1)}, u32[]{:S(2)}, u32[]{:S(2)}) %collective-permute-start.3) | collective-permute-done | bytes 184352 | tf_op jit(solution)/shard_map/ppermute | solution.py:235
  15.1 1.4 %collective-permute-done.1 = bf16[64,1152]{1,0:T(8,128)(2,1)S(1)} collective-permute-done((bf16[64,1152]{1,0:T(8,128)(2,1)S(1)}, bf16[64,1152]{1,0:T(8,128)(2,1)S(1)}, u32[]{:S(2)}, u32[]{:S(2)}) %collective-permute-start.1) | collective-permute-done | bytes 147488 | tf_op jit(solution)/shard_map/ppermute | solution.py:235
  16.5 1.2 %collective-permute-start.2 = (bf16[64,1152]{1,0:T(8,128)(2,1)S(1)}, bf16[64,1152]{1,0:T(8,128)(2,1)S(1)}, u32[]{:S(2)}, u32[]{:S(2)}) collective-permute-start(bf16[64,1152]{1,0:T(8,128)(2,1)S(1)} %get-tuple-element.38), channel_id=1, source_target_pairs={{0,4},{4,0},{8,12},{12,8},{1,5},{5,1},{9,13},{13,9},{2,6},{6,2},{1... | collective-permute-start | bytes 442376 | tf_op jit(solution)/shard_map/ppermute | solution.py:235
  17.7 4.1 %collective-permute-done.2 = bf16[64,1152]{1,0:T(8,128)(2,1)S(1)} collective-permute-done((bf16[64,1152]{1,0:T(8,128)(2,1)S(1)}, bf16[64,1152]{1,0:T(8,128)(2,1)S(1)}, u32[]{:S(2)}, u32[]{:S(2)}) %collective-permute-start.2) | collective-permute-done | bytes 147488 | tf_op jit(solution)/shard_map/ppermute | solution.py:235
  21.8 0.3 fusion.5
  22.1 1.2 %collective-permute-start.4 = (bf16[64,1152]{1,0:T(8,128)(2,1)S(1)}, bf16[64,1152]{1,0:T(8,128)(2,1)S(1)}, u32[]{:S(2)}, u32[]{:S(2)}) collective-permute-start(bf16[64,1152]{1,0:T(8,128)(2,1)S(1)} %get-tuple-element.41), channel_id=1, source_target_pairs={{0,8},{4,12},{8,0},{12,4},{1,9},{5,13},{9,1},{13,5},{2,10},{6,14},... | collective-permute-start | bytes 442376 | tf_op jit(solution)/shard_map/ppermute | solution.py:235
  23.3 1.8 %collective-permute-start.5 = (f32[1,1152]{1,0:T(1,128)S(1)}, f32[1,1152]{1,0:T(1,128)S(1)}, u32[]{:S(2)}, u32[]{:S(2)}) collective-permute-start(f32[1,1152]{1,0:T(1,128)S(1)} %get-tuple-element.44), channel_id=1, source_target_pairs={{0,8},{4,12},{8,0},{12,4},{1,9},{5,13},{9,1},{13,5},{2,10},{6,14},... | collective-permute-start | bytes 13832 | tf_op jit(solution)/shard_map/ppermute | solution.py:235
  25.1 5.7 %collective-permute-done.5.there_square_ref = f32[1,1152]{1,0:T(1,128)S(1)} collective-permute-done((f32[1,1152]{1,0:T(1,128)S(1)}, f32[1,1152]{1,0:T(1,128)S(1)}, u32[]{:S(2)}, u32[]{:S(2)}) %collective-permute-start.5) | collective-permute-done | bytes 4640 | tf_op jit(solution)/shard_map/ppermute | solution.py:235
  30.7 0.2 finish.1
  31.0 1.9 %collective-permute-start.6 = (bf16[64,1280]{1,0:T(8,128)(2,1)S(1)}, bf16[64,1280]{1,0:T(8,128)(2,1)S(1)}, u32[]{:S(2)}, u32[]{:S(2)}) collective-permute-start(bf16[64,1280]{1,0:T(8,128)(2,1)S(1)} %get-tuple-element.20.own_ref), channel_id=1, source_target_pairs={{0,2},{1,3},{2,0},{3,1},{4,6},{5,7},{6,4},{7,5},{8,10},{9,11},{10,... | collective-permute-start | bytes 491528 | tf_op jit(solution)/shard_map/ppermute | solution.py:235
  32.9 0.1 collective-permute-start.7
  33.0 0.1 pad_maximum_fusion
  33.1 1.3 %collective-permute-done.7.near_ref = bf16[64,1152]{1,0:T(8,128)(2,1)S(1)} collective-permute-done((bf16[64,1152]{1,0:T(8,128)(2,1)S(1)}, bf16[64,1152]{1,0:T(8,128)(2,1)S(1)}, u32[]{:S(2)}, u32[]{:S(2)}) %collective-permute-start.7) | collective-permute-done | bytes 147488 | tf_op jit(solution)/shard_map/ppermute | solution.py:235
  34.3 2.3 %near_gradient.1 = (f32[8,128,256]{2,1,0:T(8,128)S(1)}, bf16[3,256,1152]{2,1,0:T(8,128)(2,1)S(1)}) custom-call(s32[1,17]{1,0:T(1,128)S(4)} %get-tuple-element.17.ids_ref, bf16[64,1280]{1,0:T(8,128)(2,1)S(1)} %get-tuple-element.20.own_ref, bf16[64,1152]{1,0:T(8,128)(2,1)S(1)} %collective-permute-done.7.near_ref, bf16[2048,2304]{1,0:T(8,128)(2,1)} %bitcast.12), custom_call_target="tpu_custom_call" | custom-call | tf_op jit(solution)/shard_map/near_gradient/pallas_call | solution.py:383
  36.7 0.1 collective-permute-start.8
  36.8 0.5 %collective-permute-start.9 = (bf16[64,704]{1,0:T(8,128)(2,1)S(1)}, bf16[64,704]{1,0:T(8,128)(2,1)S(1)}, u32[]{:S(2)}, u32[]{:S(2)}) collective-permute-start(bf16[64,704]{1,0:T(8,128)(2,1)S(1)} %pad_maximum_fusion), channel_id=1, source_target_pairs={{0,1},{1,0},{2,3},{3,2},{4,5},{5,4},{6,7},{7,6},{8,9},{9,8},{10,11... | collective-permute-start | bytes 270344 | tf_op jit(solution)/shard_map/ppermute | solution.py:235
  37.3 1.0 %collective-permute-done.9.other_ref = bf16[64,704]{1,0:T(8,128)(2,1)S(1)} collective-permute-done((bf16[64,704]{1,0:T(8,128)(2,1)S(1)}, bf16[64,704]{1,0:T(8,128)(2,1)S(1)}, u32[]{:S(2)}, u32[]{:S(2)}) %collective-permute-start.9) | collective-permute-done | bytes 90144 | tf_op jit(solution)/shard_map/ppermute | solution.py:235
  38.3 2.1 %code_gradient.1 = (bf16[128,2048]{1,0:T(8,128)(2,1)}, bf16[576,128]{1,0:T(8,128)(2,1)}, f32[1,1]{1,0:T(1,128)}) custom-call(s32[1,17]{1,0:T(1,128)S(4)} %get-tuple-element.17.ids_ref, bf16[64,1280]{1,0:T(8,128)(2,1)S(1)} %get-tuple-element.20.own_ref, bf16[64,1280]{1,0:T(8,128)(2,1)S(1)} %collective-permute-done.6.got_ref, ...), custom_call_target="tpu_custom_call" | custom-call | tf_op jit(solution)/shard_map/code_gradient/pallas_call | solution.py:401
  (18 shorter events, 0.3 us)
Async XLA Ops:
  1.3 4.9 %copy-start.1 = (f32[1,2304]{1,0:T(1,128)S(1)}, f32[1,2304]{1,0:T(1,128)}, u32[]{:S(2)}) copy-start(f32[1,2304]{1,0:T(1,128)} %param.13) | copy-start | bytes 27652
  1.3 5.0 %copy-start = (bf16[1,128,2304]{2,1,0:T(8,128)(2,1)S(1)}, bf16[1,128,2304]{2,1,0:T(8,128)(2,1)}, u32[]{:S(2)}) copy-start(bf16[1,128,2304]{2,1,0:T(8,128)(2,1)} %param.9) | copy-start | bytes 1769476
  6.1 4.1 %collective-permute-start = (bf16[64,2304]{1,0:T(8,128)(2,1)S(1)}, bf16[64,2304]{1,0:T(8,128)(2,1)S(1)}, u32[]{:S(2)}, u32[]{:S(2)}) collective-permute-start(bf16[64,2304]{1,0:T(8,128)(2,1)S(1)} %get-tuple-element.19), channel_id=1, source_target_pairs={{0,1},{1,0},{2,3},{3,2},{4,5},{5,4},{6,7},{7,6},{8,9},{9,8},{10,11... | collective-permute-start | bytes 884744 | tf_op jit(solution)/shard_map/ppermute | solution.py:235
  6.8 8.3 %collective-permute-start.3 = (bf16[80,1152]{1,0:T(8,128)(2,1)S(1)}, bf16[80,1152]{1,0:T(8,128)(2,1)S(1)}, u32[]{:S(2)}, u32[]{:S(2)}) collective-permute-start(bf16[80,1152]{1,0:T(8,128)(2,1)S(1)} %concatenate.6), channel_id=1, source_target_pairs={{0,4},{4,0},{8,12},{12,8},{1,5},{5,1},{9,13},{13,9},{2,6},{6,2},{1... | collective-permute-start | bytes 552968 | tf_op jit(solution)/shard_map/ppermute | solution.py:235
  10.3 6.1 %collective-permute-start.1 = (bf16[64,1152]{1,0:T(8,128)(2,1)S(1)}, bf16[64,1152]{1,0:T(8,128)(2,1)S(1)}, u32[]{:S(2)}, u32[]{:S(2)}) collective-permute-start(bf16[64,1152]{1,0:T(8,128)(2,1)S(1)} %select_convert_fusion), channel_id=1, source_target_pairs={{0,2},{1,3},{2,0},{3,1},{4,6},{5,7},{6,4},{7,5},{8,10},{9,11},{10,... | collective-permute-start | bytes 442376 | tf_op jit(solution)/shard_map/ppermute | solution.py:235
  16.5 5.3 %collective-permute-start.2 = (bf16[64,1152]{1,0:T(8,128)(2,1)S(1)}, bf16[64,1152]{1,0:T(8,128)(2,1)S(1)}, u32[]{:S(2)}, u32[]{:S(2)}) collective-permute-start(bf16[64,1152]{1,0:T(8,128)(2,1)S(1)} %get-tuple-element.38), channel_id=1, source_target_pairs={{0,4},{4,0},{8,12},{12,8},{1,5},{5,1},{9,13},{13,9},{2,6},{6,2},{1... | collective-permute-start | bytes 442376 | tf_op jit(solution)/shard_map/ppermute | solution.py:235
  22.1 8.7 %collective-permute-start.4 = (bf16[64,1152]{1,0:T(8,128)(2,1)S(1)}, bf16[64,1152]{1,0:T(8,128)(2,1)S(1)}, u32[]{:S(2)}, u32[]{:S(2)}) collective-permute-start(bf16[64,1152]{1,0:T(8,128)(2,1)S(1)} %get-tuple-element.41), channel_id=1, source_target_pairs={{0,8},{4,12},{8,0},{12,4},{1,9},{5,13},{9,1},{13,5},{2,10},{6,14},... | collective-permute-start | bytes 442376 | tf_op jit(solution)/shard_map/ppermute | solution.py:235
  23.3 7.5 %collective-permute-start.5 = (f32[1,1152]{1,0:T(1,128)S(1)}, f32[1,1152]{1,0:T(1,128)S(1)}, u32[]{:S(2)}, u32[]{:S(2)}) collective-permute-start(f32[1,1152]{1,0:T(1,128)S(1)} %get-tuple-element.44), channel_id=1, source_target_pairs={{0,8},{4,12},{8,0},{12,4},{1,9},{5,13},{9,1},{13,5},{2,10},{6,14},... | collective-permute-start | bytes 13832 | tf_op jit(solution)/shard_map/ppermute | solution.py:235
  31.0 5.7 %collective-permute-start.6 = (bf16[64,1280]{1,0:T(8,128)(2,1)S(1)}, bf16[64,1280]{1,0:T(8,128)(2,1)S(1)}, u32[]{:S(2)}, u32[]{:S(2)}) collective-permute-start(bf16[64,1280]{1,0:T(8,128)(2,1)S(1)} %get-tuple-element.20.own_ref), channel_id=1, source_target_pairs={{0,2},{1,3},{2,0},{3,1},{4,6},{5,7},{6,4},{7,5},{8,10},{9,11},{10,... | collective-permute-start | bytes 491528 | tf_op jit(solution)/shard_map/ppermute | solution.py:235
  32.9 1.4 %collective-permute-start.7 = (bf16[64,1152]{1,0:T(8,128)(2,1)S(1)}, bf16[64,1152]{1,0:T(8,128)(2,1)S(1)}, u32[]{:S(2)}, u32[]{:S(2)}) collective-permute-start(bf16[64,1152]{1,0:T(8,128)(2,1)S(1)} %slice.32), channel_id=1, source_target_pairs={{0,1},{1,0},{2,3},{3,2},{4,5},{5,4},{6,7},{7,6},{8,9},{9,8},{10,11... | collective-permute-start | bytes 442376 | tf_op jit(solution)/shard_map/ppermute | solution.py:235
  36.7 1.6 %collective-permute-start.8 = (bf16[64,1280]{1,0:T(8,128)(2,1)S(1)}, bf16[64,1280]{1,0:T(8,128)(2,1)S(1)}, u32[]{:S(2)}, u32[]{:S(2)}) collective-permute-start(bf16[64,1280]{1,0:T(8,128)(2,1)S(1)} %collective-permute-done.6.got_ref), channel_id=1, source_target_pairs={{0,1},{1,0},{2,3},{3,2},{4,5},{5,4},{6,7},{7,6},{8,9},{9,8},{10,11... | collective-permute-start | bytes 491528 | tf_op jit(solution)/shard_map/ppermute | solution.py:235
  36.8 1.5 %collective-permute-start.9 = (bf16[64,704]{1,0:T(8,128)(2,1)S(1)}, bf16[64,704]{1,0:T(8,128)(2,1)S(1)}, u32[]{:S(2)}, u32[]{:S(2)}) collective-permute-start(bf16[64,704]{1,0:T(8,128)(2,1)S(1)} %pad_maximum_fusion), channel_id=1, source_target_pairs={{0,1},{1,0},{2,3},{3,2},{4,5},{5,4},{6,7},{7,6},{8,9},{9,8},{10,11... | collective-permute-start | bytes 270344 | tf_op jit(solution)/shard_map/ppermute | solution.py:235
